TPU v7x, 512 devices: a whole 4x8x8 slice. The times are simulated.
512 devices in a mesh: space: 16 (over z, core), member: 8 (over y), tm: 4 (over x).
Axes of the slice: x: 4, y: 8, z: 8, core: 2. Of those that a mesh axis runs over, the one named last changes fastest.
Arguments:
- ens_pert: bfloat16 [8, 128, 131072], P('tm', 'member', 'space'), may hold values from -6 to 6
- weights: float32 [128, 512], P('member', 'space'), may hold values from -6 to 6
- foot_block: int32 [8, 16, 16, 8, 32], P('tm', 'space'), may hold values from 0 to 31
- foot_offset: int32 [8, 16, 16, 8, 32], P('tm', 'space'), may hold values from 0 to 255
- innovation: float32 [8, 16, 8, 16, 32], P('tm', 'space', 'member'), may hold values from -6 to 6
- inv_var: float32 [8, 16, 8, 16, 32], P('tm', 'space', 'member'), may hold values from 0.25 to 2.5
- obs_count: int32 [8, 16, 8, 16], P('tm', 'space', 'member'), may hold values from 1 to 32, as said below
Outputs:
- gradient: float32 [128, 512], P('member', 'space')
Inputs may be any that keep to these rules, and one draw needn't show every extreme that they name: `obs_count`: live slots come first among the 32 slots; in every time slot one destination tile has all 32 slots live from every owner.
All inputs are finite; a program needn't handle non-finite values.
Results may differ from a plain program's by a relative error of at most 0.0029.
Values sent between devices are 32-bit elements; how exact they have to be, the bound alone decides.
No kernel may reach another device: no remote copies, remote signals or barrier semaphores. Data moves between devices by JAX's collectives and lax.ppermute only.
A program may use at most 64 MiB of HBM per device.

v0:
```python
import math

import jax
import jax.numpy as jnp
from jax import lax
from jax.sharding import PartitionSpec as P

BLOCK = 256


def split_pair(values, axis_at):
    upper = lax.optimization_barrier(values.astype(jnp.bfloat16))
    lower = (values - upper.astype(jnp.float32)).astype(jnp.bfloat16)
    return jnp.concatenate([upper, lower], axis=axis_at)


def shards(ens_pert, weights, foot_block, foot_offset, innovation, inv_var, obs_count):
    tile_count = lax.axis_size("space")
    group_count = lax.axis_size("member")
    slot_count, members, cell_dev = ens_pert.shape
    capacity = foot_block.shape[-1]
    blk_dev = cell_dev // BLOCK
    norm_scale = 1.0 / math.sqrt(members * group_count - 1)
    pert_blocks = ens_pert.reshape(slot_count, members, blk_dev, BLOCK)
    weights_rounded = weights.astype(jnp.bfloat16)
    partial_field = norm_scale * jnp.einsum(
        "tmbc,mb->tbc", pert_blocks, weights_rounded, preferred_element_type=jnp.float32
    )
    split_field = split_pair(partial_field, 1)
    block_rows = jnp.transpose(foot_block.reshape(slot_count, tile_count, -1), (1, 0, 2))
    offset_rows = jnp.transpose(foot_offset.reshape(slot_count, tile_count, -1), (1, 0, 2))
    block_iota = lax.broadcasted_iota(jnp.int32, (1, blk_dev, 1), 1)
    offset_iota = lax.broadcasted_iota(jnp.int32, (1, 1, BLOCK), 2)

    def pick_tile(pair):
        blk_ids, off_ids = pair
        off_hot = (off_ids[:, :, None] == offset_iota).astype(jnp.bfloat16)
        proj = jnp.einsum("tjc,tkc->tjk", split_field, off_hot, preferred_element_type=jnp.float32)
        value = proj[:, :blk_dev] + proj[:, blk_dev:]
        chosen = jnp.where(blk_ids[:, None, :] == block_iota, value, jnp.zeros_like(value))
        return jnp.sum(chosen, axis=1)

    picked = jnp.transpose(lax.map(pick_tile, (block_rows, offset_rows)), (1, 0, 2))
    arrived_vals = lax.all_to_all(
        picked.reshape(slot_count, tile_count * group_count, capacity),
        ("space", "member"),
        split_axis=1,
        concat_axis=1,
        tiled=True,
    )
    model_obs = jnp.sum(arrived_vals.reshape(slot_count, tile_count, group_count, capacity), axis=2)
    innov_local = innovation.reshape(slot_count, tile_count, capacity)
    obs_weight = inv_var.reshape(slot_count, tile_count, capacity)
    counts = obs_count.reshape(slot_count, tile_count, 1)
    is_live = lax.broadcasted_iota(jnp.int32, (slot_count, tile_count, capacity), 2) < counts
    residual = jnp.where(
        is_live, obs_weight * (model_obs - innov_local), jnp.zeros_like(innov_local)
    )
    residual = residual.reshape(slot_count, 1, 1, tile_count, capacity)
    spread = lax.all_gather(residual, "member", axis=2, tiled=True)
    arrived = lax.all_to_all(spread, "space", split_axis=3, concat_axis=1, tiled=True)
    arrived_rows = jnp.transpose(arrived.reshape(slot_count, tile_count, -1), (1, 0, 2))

    def add_tile(total, triple):
        blk_ids, off_ids, values = triple
        off_hot = (off_ids[:, :, None] == offset_iota).astype(jnp.bfloat16)
        placed = jnp.where(
            blk_ids[:, None, :] == block_iota, values[:, None, :], jnp.zeros((), jnp.float32)
        )
        both = split_pair(placed, 1)
        part_sum = jnp.einsum("tjk,tkc->tjc", both, off_hot, preferred_element_type=jnp.float32)
        return (total + (part_sum[:, :blk_dev] + part_sum[:, blk_dev:]), None)

    start_total = jnp.zeros((slot_count, blk_dev, BLOCK), jnp.float32)
    adjoint, _ = lax.scan(add_tile, start_total, (block_rows, offset_rows, arrived_rows))
    adjoint_rounded = adjoint.astype(jnp.bfloat16)
    local_grad = jnp.einsum(
        "tmbc,tbc->mb", pert_blocks, adjoint_rounded, preferred_element_type=jnp.float32
    )
    summed = lax.psum(local_grad, "tm")
    return weights + norm_scale * summed


def solution(mesh):
    in_specs = (
        P("tm", "member", "space"),
        P("member", "space"),
        P("tm", "space", None, None, None),
        P("tm", "space", None, None, None),
        P("tm", "space", "member", None, None),
        P("tm", "space", "member", None, None),
        P("tm", "space", "member", None),
    )
    out_specs = P("member", "space")
    return jax.shard_map(shards, mesh=mesh, in_specs=in_specs, out_specs=out_specs, check_vma=False)
```

profile of v0, /device:TPU:1, one launch (start us, length us, event | category | flops | bytes accessed | tf_op | source)
XLA Modules:
  0.0 95.3 jit_solution(16273810836954491873)
XLA Ops:
  0.0 0.7 convert_bitcast_fusion.1
  0.7 0.1 copy.38
  0.8 1.2 %fusion.21 = f32[32,1,2,256]{3,1,2,0:T(1,128)S(1)} fusion(bf16[16,32,1,1]{0,2,3,1:T(2,128)(2,1)S(1)} %copy.38, bf16[2,2,32,8,256]{4,3,2,1,0:T(8,128)(2,1)} %bitcast.84), kind=kOutput, calls=%fused_computation.32 | convolution fusion | flops 524288 | bytes 590848 | tf_op jit(solution)/shard_map/tmbc,mb->tbc/dot_general | solution.py:26
  2.1 0.0 copy-start.1
  2.1 0.0 copy-start.2
  2.1 0.8 copy-done.1
  3.0 0.1 reshape.52
  3.1 0.1 reshape.53
  3.2 0.1 copy_bitcast_fusion
  3.2 5.8 %while.22 = (s32[]{:T(128)}, f32[16,2,256]{2,1,0:T(2,128)S(1)}, s32[16,2,256]{2,1,0:T(2,128)S(1)}, s32[16,2,256]{2,1,0:T(2,128)S(1)}, bf16[2,64,256]{2,1,0:T(8,128)(2,1)S(1)}, /*index=5*/s32[]{:T(128)}) while((s32[]{:T(128)}, f32[16,2,256]{2,1,0:T(2,128)S(1)}, s32[16,2,256]{2,1,0:T(2,128)S(1)}, s32[16,2,256]{2,1,0:T(2,128)S(1)}, ...), condition=%wide.region_2.3_spmd.clone, body=%wide.region_0.2_spmd.clone.sunk | while | flops 16973312 | bytes 346189 | solution.py:43
  3.3 0.3 convolution_bitcast_fusion.2
  3.6 0.3 convolution_bitcast_fusion.2
  4.0 0.3 convolution_bitcast_fusion.2
  4.3 0.3 convolution_bitcast_fusion.2
  4.7 0.3 convolution_bitcast_fusion.2
  5.1 0.3 convolution_bitcast_fusion.2
  5.4 0.3 convolution_bitcast_fusion.2
  5.8 0.3 convolution_bitcast_fusion.2
  6.2 0.3 convolution_bitcast_fusion.2
  6.5 0.3 convolution_bitcast_fusion.2
  6.9 0.3 convolution_bitcast_fusion.2
  7.2 0.3 convolution_bitcast_fusion.2
  7.6 0.3 convolution_bitcast_fusion.2
  8.0 0.3 convolution_bitcast_fusion.2
  8.3 0.3 convolution_bitcast_fusion.2
  8.7 0.3 convolution_bitcast_fusion.2
  9.0 0.1 reshape.45
  9.1 0.8 copy.33
  9.9 18.4 %all-to-all-start = ((f32[2,128,32]{2,0,1:T(2,128)}), f32[2,128,32]{2,0,1:T(2,128)S(1)}, u32[]{:S(2)}, u32[]{:S(2)}) async-start(f32[2,128,32]{2,0,1:T(2,128)} %copy.33), calls=%async_computation | async-start | bytes 262144 | tf_op jit(solution)/shard_map/all_to_all | solution.py:44
  28.3 0.7 copy-done.6
  29.0 0.1 copy.30
  29.1 11.8 %all-to-all-done = f32[2,128,32]{2,0,1:T(2,128)S(1)} async-done(((f32[2,128,32]{2,0,1:T(2,128)}), f32[2,128,32]{2,0,1:T(2,128)S(1)}, u32[]{:S(2)}, u32[]{:S(2)}) %all-to-all-start) | async-done | bytes 32800 | tf_op jit(solution)/shard_map/all_to_all | solution.py:44
  40.9 0.1 compare_select_fusion
  41.0 18.2 %all_gather.3 = f32[2,1,8,16,32]{4,3,1,0,2:T(8,128)S(1)} all-gather(f32[2,1,1,16,32]{4,3,1,0,2:T(8,128)S(1)} %copy.36), channel_id=1, replica_groups=mesh['space'=16,'member'=8,'tm'=4] {'member'}, dimensions={2}, use_global_device_ids=true | all-gather | bytes 36864 | tf_op jit(solution)/shard_map/all_gather | solution.py:60
  59.3 0.1 copy.66
  59.4 0.7 reshape.54
  60.1 10.0 %all-to-all-start.1 = ((f32[16,1,512]{2,1,0:T(1,128)}), f32[16,1,512]{2,1,0:T(1,128)S(1)}, u32[]{:S(2)}, u32[]{:S(2)}) async-start(f32[16,1,512]{2,1,0:T(1,128)} %reshape.54), calls=%async_computation.1 | async-start | bytes 65536 | tf_op jit(solution)/shard_map/all_to_all | solution.py:61
  70.1 7.5 %all-to-all-done.1 = f32[16,1,512]{2,1,0:T(1,128)S(1)} async-done(((f32[16,1,512]{2,1,0:T(1,128)}), f32[16,1,512]{2,1,0:T(1,128)S(1)}, u32[]{:S(2)}, u32[]{:S(2)}) %all-to-all-start.1) | async-done | bytes 32800 | tf_op jit(solution)/shard_map/all_to_all | solution.py:61
  77.6 0.5 broadcast.27
  78.1 0.7 reduce
  78.8 0.1 reshape.55
  78.9 0.1 reshape.47
  79.0 0.0 copy-start
  79.0 6.6 %while.23 = (s32[]{:T(128)}, f32[2,32,256]{2,1,0:T(8,128)S(1)}, s32[16,2,256]{2,1,0:T(2,128)S(1)}, f32[16,2,256]{2,1,0:T(2,128)S(1)}, s32[16,2,256]{2,1,0:T(2,128)S(1)}, /*index=5*/s32[]{:T(128)}, s32[]{:T(128)}) while((s32[]{:T(128)}, f32[2,32,256]{2,1,0:T(8,128)S(1)}, s32[16,2,256]{2,1,0:T(2,128)S(1)}, ...), condition=%wide.region_5.6_spmd.clone, body=%wide.region_4.5_spmd.clone.sunk | while | flops 17203200 | bytes 579679 | solution.py:75
  79.1 0.3 fusion.40
  79.5 0.3 fusion.40
  80.0 0.3 fusion.40
  80.4 0.3 fusion.40
  80.8 0.3 fusion.40
  81.2 0.3 fusion.40
  81.6 0.3 fusion.40
  82.0 0.3 fusion.40
  82.4 0.3 fusion.40
  82.8 0.3 fusion.40
  83.2 0.3 fusion.40
  83.7 0.3 fusion.40
  84.1 0.3 fusion.40
  84.5 0.3 fusion.40
  84.9 0.3 fusion.40
  85.3 0.3 fusion.40
  85.7 0.3 fusion.19
  85.9 0.1 copy.42
  86.0 8.7 %psum.7 = f32[16,32]{1,0:T(8,128)S(1)} all-reduce(f32[16,32]{1,0:T(8,128)S(1)} %bitcast.88), channel_id=1, replica_groups=mesh['space'=16,'member'=8,'tm'=4] {'tm'}, use_global_device_ids=true, to_apply=%region_6.7 | all-reduce | flops 512 | bytes 4096 | tf_op jit(solution)/shard_map/psum | solution.py:80
  94.7 0.6 multiply_add_fusion
  (147 shorter events, 2.1 us)
Async XLA Ops:
  2.1 0.9 copy-start.1
  2.1 1.0 %copy-start.2 = (s32[2,1,16,8,32]{4,3,2,1,0:T(8,128)S(1)}, s32[2,1,16,8,32]{4,3,2,1,0:T(8,128)}, u32[]{:S(2)}) copy-start(s32[2,1,16,8,32]{4,3,2,1,0:T(8,128)} %param.14) | copy-start | bytes 98308
  9.9 31.0 %all-to-all-start = ((f32[2,128,32]{2,0,1:T(2,128)}), f32[2,128,32]{2,0,1:T(2,128)S(1)}, u32[]{:S(2)}, u32[]{:S(2)}) async-start(f32[2,128,32]{2,0,1:T(2,128)} %copy.33), calls=%async_computation | async-start | bytes 262144 | tf_op jit(solution)/shard_map/all_to_all | solution.py:44
  28.3 0.7 copy-start.6
  29.1 11.8 %copy-start.4 = (f32[2,1,1,16,32]{4,3,2,1,0:T(8,128)S(1)}, f32[2,1,1,16,32]{4,3,2,1,0:T(8,128)}, u32[]{:S(2)}) copy-start(f32[2,1,1,16,32]{4,3,2,1,0:T(8,128)} %param.16) | copy-start | bytes 12292
  29.1 11.8 %copy-start.5 = (f32[2,1,1,16,32]{4,3,2,1,0:T(8,128)S(1)}, f32[2,1,1,16,32]{4,3,2,1,0:T(8,128)}, u32[]{:S(2)}) copy-start(f32[2,1,1,16,32]{4,3,2,1,0:T(8,128)} %param.15) | copy-start | bytes 12292
  60.1 17.5 %all-to-all-start.1 = ((f32[16,1,512]{2,1,0:T(1,128)}), f32[16,1,512]{2,1,0:T(1,128)S(1)}, u32[]{:S(2)}, u32[]{:S(2)}) async-start(f32[16,1,512]{2,1,0:T(1,128)} %reshape.54), calls=%async_computation.1 | async-start | bytes 65536 | tf_op jit(solution)/shard_map/all_to_all | solution.py:61
  79.0 6.6 %copy-start = (bf16[2,16,8192]{2,1,0:T(8,128)(2,1)S(1)}, bf16[2,16,8192]{2,1,0:T(8,128)(2,1)}, u32[]{:S(2)}) copy-start(bf16[2,16,8192]{2,1,0:T(8,128)(2,1)} %param.11) | copy-start | bytes 1572868
  86.0 8.7 %copy-start.3 = (f32[16,32]{1,0:T(8,128)S(1)}, f32[16,32]{1,0:T(8,128)}, u32[]{:S(2)}) copy-start(f32[16,32]{1,0:T(8,128)} %param.12) | copy-start | bytes 6148
where the time goes:
time: 95.7 us; the launch traced here: 95.3 us
  starting transfers between devices  28.4 us (30%)
  blocking collectives  26.9 us (28%)
  waiting for transfers between devices  19.2 us (20%)
  matrix products  10.3 us (11%)
  local copies, waits for them, and re-layouts  5.06 us (5%)
  other arithmetic  3.52 us (4%)
  loops' own time  1.59 us (2%)
    all_to_all x1, starting transfers between devices, shards(): lax.all_to_all(picked.reshape(slot_count, tile_count * group_count, capac...  18.4 us
    all_gather x1, blocking collectives, shards(): spread = lax.all_gather(residual, 'member', axis=2, tiled=True)  18.2 us
    all_to_all x1, waiting for transfers between devices, shards(): lax.all_to_all(picked.reshape(slot_count, tile_count * group_count, capac...  11.8 us
    all_to_all x1, starting transfers between devices, shards(): lax.all_to_all(spread, 'space', split_axis=3, concat_axis=1, tiled=True)  10 us
    psum x1, blocking collectives, shards(): summed = lax.psum(local_grad, 'tm')  8.7 us
    all_to_all x1, waiting for transfers between devices, shards(): lax.all_to_all(spread, 'space', split_axis=3, concat_axis=1, tiled=True)  7.48 us
    dot_general x16, matrix products, add_tile(): jnp.einsum('tjk,tkc->tjc', both, off_hot, preferred_element_type=jnp.floa...  4.45 us
    dot_general x16, matrix products, pick_tile(): jnp.einsum('tjc,tkc->tjk', split_field, off_hot, preferred_element_type=j...  4.35 us
  transfers between devices with their start and end apart: 2, of which 2 were waited for; matrix products, arithmetic and copies ran while one was open for 0% of the time, Pallas kernels for 0%

commit v1 on v0

v1 whole, which is shorter than its diff:
```python
import math

import jax
import jax.numpy as jnp
from jax import lax
from jax.experimental import pallas as pl
from jax.experimental.pallas import tpu as pltpu
from jax.sharding import PartitionSpec as P

BLOCK = 256
VMEM = pl.BlockSpec(memory_space=pltpu.VMEM)
PARAMS = pltpu.CompilerParams(vmem_limit_bytes=32 * 1024 * 1024)
F32, BF16 = jnp.float32, jnp.bfloat16
NT = (((1,), (1,)), ((), ()))


def owned_kernel(innov_ref, var_ref, count_ref, out_ref):
    slots, tiles, cap = innov_ref.shape
    diag = lax.broadcasted_iota(jnp.int32, (tiles, tiles), 0) == lax.broadcasted_iota(
        jnp.int32, (tiles, tiles), 1
    )
    lane = lax.broadcasted_iota(jnp.int32, (tiles, cap), 1).astype(F32)
    for t in range(slots):
        row = count_ref[t : t + 1, :].astype(F32)
        column = jnp.sum(jnp.where(diag, row, 0.0), axis=1, keepdims=True)
        w = jnp.where(lane < column, var_ref[t], 0.0)
        out_ref[:, t * cap : (t + 1) * cap] = w
        out_ref[:, (slots + t) * cap : (slots + t + 1) * cap] = w * innov_ref[t]


def pick_kernel(scale, ens_ref, w_ref, fb_ref, fo_ref, pick_ref, fbr_ref, for_ref, field, split):
    slots, members, cells = ens_ref.shape
    blocks = cells // BLOCK
    tiles, groups, cap = fb_ref.shape[1:]
    quarters = 128 // cap
    a_rows = tiles // quarters
    for t in range(slots):
        for a in range(tiles):
            rows = pl.ds((t * a_rows + a % a_rows) * groups, groups)
            lanes = slice((a // a_rows) * cap, (a // a_rows + 1) * cap)
            fbr_ref[rows, lanes] = fb_ref[t, a]
            for_ref[rows, lanes] = fo_ref[t, a]
    w = w_ref[...].astype(BF16).astype(F32)
    for b in range(blocks):
        column = w[:, b : b + 1]
        for t in range(slots):
            e = ens_ref[t, :, b * BLOCK : (b + 1) * BLOCK].astype(F32)
            field[t, b : b + 1, :] = jnp.sum(e * column, axis=0, keepdims=True)
    for t in range(slots):
        f = field[t] * scale
        upper = f.astype(BF16)
        split[t, :blocks, :] = upper
        split[t, blocks:, :] = (f - upper.astype(F32)).astype(BF16)
    off_iota = lax.broadcasted_iota(jnp.int32, (BLOCK, 128), 0)
    blk_iota = lax.broadcasted_iota(jnp.int32, (blocks, 128), 0)
    per_slot = a_rows * groups

    @pl.loop(0, slots * a_rows)
    def _(step):
        base = pl.multiple_of(step * 8, 8)
        off = for_ref[pl.ds(base, 8), :]
        blk = fbr_ref[pl.ds(base, 8), :]
        hot = jnp.concatenate(
            [(off_iota == off[r : r + 1]).astype(F32).astype(BF16) for r in range(8)], axis=1
        )
        lhs = split[step // a_rows]
        proj = jnp.dot(lhs, hot, preferred_element_type=F32)
        value = proj[:blocks] + proj[blocks:]
        picked = [
            jnp.sum(
                jnp.where(blk_iota == blk[r : r + 1], value[:, r * 128 : (r + 1) * 128], 0.0),
                axis=0,
                keepdims=True,
            )
            for r in range(8)
        ]
        pick_ref[pl.ds(base, 8), :] = jnp.concatenate(picked, axis=0)


def join_kernel(pick_ref, owned_ref, out_ref):
    rows = pick_ref.shape[0]
    for peer in range(out_ref.shape[0]):
        out_ref[peer, :rows, :] = pick_ref[...]
        out_ref[peer, rows:, :] = owned_ref[...]


def gradient_kernel(ens_ref, got_ref, fbr_ref, for_ref, out_ref, res):
    slots, members, cells = ens_ref.shape
    blocks = cells // BLOCK
    groups = got_ref.shape[0]
    rows = fbr_ref.shape[0]
    tiles = got_ref.shape[1] - rows
    a_rows = rows // (slots * groups)
    quarters = tiles // a_rows
    cap = 128 // quarters
    quarter = lax.broadcasted_iota(jnp.int32, (groups, 128), 1) // cap

    def aligned(message, source, target):
        shift = (target - source) * cap % 128
        return pltpu.roll(message, shift, 1) if shift else message

    for a in range(a_rows):
        messages = [got_ref[:, rows + a + q * a_rows, :] for q in range(quarters)]
        for t in range(slots):
            w = jnp.zeros((groups, 128), F32)
            d = jnp.zeros((groups, 128), F32)
            for q in range(quarters):
                w = jnp.where(quarter == q, aligned(messages[q], t, q), w)
                d = jnp.where(quarter == q, aligned(messages[q], slots + t, q), d)
            at = pl.ds((t * a_rows + a) * groups, groups)
            x = got_ref[0, at, :]
            for peer in range(1, groups):
                x = x + got_ref[peer, at, :]
            res[at, :] = w * x - d
    off_iota = lax.broadcasted_iota(jnp.int32, (BLOCK, 128), 0)
    blk_iota = lax.broadcasted_iota(jnp.int32, (blocks, 128), 0)
    local = None
    for t in range(slots):

        def add_rows(step, total, t=t):
            base = pl.multiple_of((t * a_rows + step) * 8, 8)
            off = for_ref[pl.ds(base, 8), :]
            blk = fbr_ref[pl.ds(base, 8), :]
            value = res[pl.ds(base, 8), :]
            hot = jnp.concatenate(
                [(off_iota == off[r : r + 1]).astype(F32).astype(BF16) for r in range(8)], axis=1
            )
            placed = jnp.concatenate(
                [jnp.where(blk_iota == blk[r : r + 1], value[r : r + 1], 0.0) for r in range(8)],
                axis=1,
            )
            upper = placed.astype(BF16)
            lower = (placed - upper.astype(F32)).astype(BF16)
            both = jnp.concatenate([upper, lower], axis=0)
            return total + lax.dot_general(both, hot, NT, preferred_element_type=F32)

        total = lax.fori_loop(0, a_rows, add_rows, jnp.zeros((2 * blocks, BLOCK), F32))
        adjoint = (total[:blocks] + total[blocks:]).astype(BF16)
        lhs = jnp.concatenate(
            [ens_ref[t, :, b * BLOCK : (b + 1) * BLOCK] for b in range(blocks)], axis=0
        )
        prod = lax.dot_general(lhs, adjoint, NT, preferred_element_type=F32)
        part = prod.reshape(blocks, members, blocks)
        own = lax.broadcasted_iota(jnp.int32, part.shape, 0) == lax.broadcasted_iota(
            jnp.int32, part.shape, 2
        )
        part = jnp.sum(jnp.where(own, part, 0.0), axis=0)
        local = part if local is None else local + part
    padded = jnp.concatenate([local, jnp.zeros((members, 128 - blocks), F32)], axis=1)
    for peer in range(out_ref.shape[0]):
        out_ref[peer] = padded


def finish_kernel(scale, got_ref, w_ref, out_ref):
    total = got_ref[0]
    for peer in range(1, got_ref.shape[0]):
        total = total + got_ref[peer]
    out_ref[...] = w_ref[...] + scale * total[:, : w_ref.shape[1]]


def cost(flops, read):
    return pl.CostEstimate(flops=flops, bytes_accessed=read, transcendentals=0)


def shards(ens_pert, weights, foot_block, foot_offset, innovation, inv_var, obs_count):
    groups = lax.axis_size("member")
    windows = lax.axis_size("tm")
    slots, members, cells = ens_pert.shape
    blocks = cells // BLOCK
    tiles, _, cap = foot_block.shape[2:]
    rows = slots * tiles * groups * cap // 128
    scale = 1.0 / math.sqrt(members * groups - 1)
    foot_block = foot_block.reshape(slots, tiles, groups, cap)
    foot_offset = foot_offset.reshape(slots, tiles, groups, cap)
    owned = pl.pallas_call(
        owned_kernel,
        out_shape=jax.ShapeDtypeStruct((tiles, 128), F32),
        in_specs=[VMEM] * 3,
        out_specs=VMEM,
        compiler_params=PARAMS,
    )(
        innovation.reshape(slots, tiles, cap),
        inv_var.reshape(slots, tiles, cap),
        obs_count.reshape(slots, tiles),
    )
    owned = lax.all_to_all(owned, "space", 0, 0, tiled=True)
    pairs = 2 * blocks * rows * 128 * BLOCK
    picks, fbr, offr = pl.pallas_call(
        lambda *refs: pick_kernel(scale, *refs),
        out_shape=(
            jax.ShapeDtypeStruct((rows, 128), F32),
            jax.ShapeDtypeStruct((rows, 128), jnp.int32),
            jax.ShapeDtypeStruct((rows, 128), jnp.int32),
        ),
        in_specs=[VMEM] * 4,
        out_specs=(VMEM,) * 3,
        scratch_shapes=[
            pltpu.VMEM((slots, blocks, BLOCK), F32),
            pltpu.VMEM((slots, 2 * blocks, BLOCK), BF16),
        ],
        compiler_params=PARAMS,
        cost_estimate=cost(2 * pairs, 2 << 20),
    )(ens_pert, weights, foot_block, foot_offset)
    joined = pl.pallas_call(
        join_kernel,
        out_shape=jax.ShapeDtypeStruct((groups, rows + tiles, 128), F32),
        in_specs=[VMEM] * 2,
        out_specs=VMEM,
        compiler_params=PARAMS,
    )(picks, owned)
    got = lax.all_to_all(joined, "member", 0, 0, tiled=True)
    local = pl.pallas_call(
        gradient_kernel,
        out_shape=jax.ShapeDtypeStruct((windows, members, 128), F32),
        in_specs=[VMEM] * 4,
        out_specs=VMEM,
        scratch_shapes=[pltpu.VMEM((rows, 128), F32)],
        compiler_params=PARAMS,
    )(ens_pert, got, fbr, offr)
    parts = lax.all_to_all(local, "tm", 0, 0, tiled=True)
    return pl.pallas_call(
        lambda *refs: finish_kernel(scale, *refs),
        out_shape=jax.ShapeDtypeStruct(weights.shape, F32),
        in_specs=[VMEM] * 2,
        out_specs=VMEM,
        compiler_params=PARAMS,
    )(parts, weights)


def solution(mesh):
    in_specs = (
        P("tm", "member", "space"),
        P("member", "space"),
        P("tm", "space", None, None, None),
        P("tm", "space", None, None, None),
        P("tm", "space", "member", None, None),
        P("tm", "space", "member", None, None),
        P("tm", "space", "member", None),
    )
    out_specs = P("member", "space")
    return jax.shard_map(shards, mesh=mesh, in_specs=in_specs, out_specs=out_specs, check_vma=False)
```

time: 95.7 us -> 53.7 us (0.56)
  the two profiles are of different devices: /device:TPU:1 before, /device:TPU:2 now
where the time goes in v1:
time: 53.7 us; the launch traced here: 53.3 us
  blocking collectives  28.8 us (54%)
  starting transfers between devices  10.6 us (20%)
  Pallas kernels  6.44 us (12%)
  local copies, waits for them, and re-layouts  4.97 us (9%)
  waiting for transfers between devices  2.47 us (5%)
    all_to_all x1, blocking collectives, shards(): got = lax.all_to_all(joined, 'member', 0, 0, tiled=True)  20.2 us
    all_to_all x1, starting transfers between devices, shards(): owned = lax.all_to_all(owned, 'space', 0, 0, tiled=True)  10.6 us
    all_to_all x1, blocking collectives, shards(): parts = lax.all_to_all(local, 'tm', 0, 0, tiled=True)  8.62 us
    unnamed x16, local copies, waits for them, and re-layouts  4.97 us
    pallas_call x1, Pallas kernels, shards(): pl.pallas_call(gradient_kernel, out_shape=jax.ShapeDtypeStruct((windows,...  2.92 us
    all_to_all x1, waiting for transfers between devices, shards(): owned = lax.all_to_all(owned, 'space', 0, 0, tiled=True)  2.47 us
    pallas_call x1, Pallas kernels, shards(): pl.pallas_call(lambda *refs: pick_kernel(scale, *refs), out_shape=(jax.Sh...  2.14 us
  transfers between devices with their start and end apart: 1, of which 1 were waited for; matrix products, arithmetic and copies ran while one was open for 0% of the time, Pallas kernels for 4%

profile of v1, /device:TPU:2, one launch (start us, length us, event | category | flops | bytes accessed | tf_op | source)
XLA Modules:
  0.0 53.3 jit_solution(13212089391945691134)
XLA Ops:
  0.0 0.0 copy-start.5
  0.0 0.7 %copy-done.5 = s32[2,1,1,16]{3,2,1,0:T(1,128)S(1)} copy-done((s32[2,1,1,16]{3,2,1,0:T(1,128)S(1)}, s32[2,1,1,16]{3,2,1,0:T(1,128)}, u32[]{:S(2)}) %copy-start.5) | copy-done | bytes 152
  0.7 0.0 copy-start.2
  0.7 0.7 %copy-done.2 = f32[2,1,1,16,32]{4,3,2,1,0:T(8,128)S(1)} copy-done((f32[2,1,1,16,32]{4,3,2,1,0:T(8,128)S(1)}, f32[2,1,1,16,32]{4,3,2,1,0:T(8,128)}, u32[]{:S(2)}) %copy-start.2) | copy-done | bytes 4120
  1.4 0.0 copy-start.3
  1.4 0.7 %copy-done.3 = f32[2,1,1,16,32]{4,3,2,1,0:T(8,128)S(1)} copy-done((f32[2,1,1,16,32]{4,3,2,1,0:T(8,128)S(1)}, f32[2,1,1,16,32]{4,3,2,1,0:T(8,128)}, u32[]{:S(2)}) %copy-start.3) | copy-done | bytes 4120
  2.1 0.8 %shard_map.74 = f32[16,128]{1,0:T(8,128)} custom-call(f32[2,16,32]{2,1,0:T(8,128)S(1)} %bitcast.10, f32[2,16,32]{2,1,0:T(8,128)S(1)} %bitcast.11, s32[2,16]{1,0:T(2,128)S(1)} %bitcast.12), custom_call_target="tpu_custom_call" | custom-call | tf_op jit(solution)/shard_map/pallas_call | solution.py:175
  2.9 0.0 copy-start.4
  2.9 10.6 %all-to-all-start = ((f32[16,1,128]{2,1,0:T(1,128)}), f32[16,1,128]{2,1,0:T(1,128)S(1)}, u32[]{:S(2)}, u32[]{:S(2)}) async-start(f32[16,1,128]{2,1,0:T(1,128)} %bitcast.6), calls=%async_computation | async-start | bytes 16384 | tf_op jit(solution)/shard_map/all_to_all | solution.py:186
  13.4 0.0 copy-done.4
  13.4 0.0 copy-start
  13.5 1.0 %copy-done = bf16[2,16,8192]{2,1,0:T(8,128)(2,1)S(1)} copy-done((bf16[2,16,8192]{2,1,0:T(8,128)(2,1)S(1)}, bf16[2,16,8192]{2,1,0:T(8,128)(2,1)}, u32[]{:S(2)}) %copy-start) | copy-done | bytes 524312
  14.5 0.0 copy-start.6
  14.5 0.9 %copy-done.6 = s32[2,1,16,8,32]{4,3,2,1,0:T(8,128)S(1)} copy-done((s32[2,1,16,8,32]{4,3,2,1,0:T(8,128)S(1)}, s32[2,1,16,8,32]{4,3,2,1,0:T(8,128)}, u32[]{:S(2)}) %copy-start.6) | copy-done | bytes 32792
  15.4 0.0 copy-start.7
  15.4 0.9 %copy-done.7 = s32[2,1,16,8,32]{4,3,2,1,0:T(8,128)S(1)} copy-done((s32[2,1,16,8,32]{4,3,2,1,0:T(8,128)S(1)}, s32[2,1,16,8,32]{4,3,2,1,0:T(8,128)}, u32[]{:S(2)}) %copy-start.7) | copy-done | bytes 32792
  16.3 2.1 %shard_map.73 = (f32[64,128]{1,0:T(8,128)S(1)}, s32[64,128]{1,0:T(8,128)S(1)}, s32[64,128]{1,0:T(8,128)S(1)}) custom-call(bf16[2,16,8192]{2,1,0:T(8,128)(2,1)S(1)} %copy-done, f32[16,32]{1,0:T(8,128)S(1)} %copy-done.4, s32[2,16,8,32]{3,2,1,0:T(8,128)S(1)} %bitcast.13, s32[2,16,8,32]{3,2,1,0:T(8,128)S(1)} %bitcast.14), custom_call_target="tpu_custom_call" | custom-call | flops 268435456 | bytes 2097152 | tf_op jit(solution)/shard_map/pallas_call | solution.py:188
  18.4 0.0 copy-start.1
  18.5 2.5 %all-to-all-done = f32[16,1,128]{2,1,0:T(1,128)S(1)} async-done(((f32[16,1,128]{2,1,0:T(1,128)}), f32[16,1,128]{2,1,0:T(1,128)S(1)}, u32[]{:S(2)}, u32[]{:S(2)}) %all-to-all-start) | async-done | bytes 8224 | tf_op jit(solution)/shard_map/all_to_all | solution.py:186
  21.0 20.2 %all_to_all.21.got_ref = f32[8,80,128]{2,1,0:T(8,128)S(1)} all-to-all(f32[8,80,128]{2,1,0:T(8,128)S(1)} %shard_map.75), channel_id=1, replica_groups=mesh['space'=16,'member'=8,'tm'=4] {'member'}, dimensions={0} | all-to-all | bytes 655360 | tf_op jit(solution)/shard_map/all_to_all | solution.py:211
  41.2 0.0 copy-done.1
  41.2 2.9 %shard_map.76 = f32[4,16,128]{2,1,0:T(8,128)S(1)} custom-call(bf16[2,16,8192]{2,1,0:T(8,128)(2,1)S(1)} %copy-done.1, f32[8,80,128]{2,1,0:T(8,128)S(1)} %all_to_all.21.got_ref, s32[64,128]{1,0:T(8,128)S(1)} %get-tuple-element.9.fbr_ref, s32[64,128]{1,0:T(8,128)S(1)} %get-tuple-element.10.for_ref), custom_call_target="tpu_custom_call" | custom-call | tf_op jit(solution)/shard_map/pallas_call | solution.py:212
  44.1 8.6 %all_to_all.22.refs_0_ = f32[4,16,128]{2,1,0:T(8,128)S(1)} all-to-all(f32[4,16,128]{2,1,0:T(8,128)S(1)} %shard_map.76), channel_id=1, replica_groups=mesh['space'=16,'member'=8,'tm'=4] {'tm'}, dimensions={0} | all-to-all | bytes 65536 | tf_op jit(solution)/shard_map/all_to_all | solution.py:220
  52.7 0.6 %shard_map.77 = f32[16,32]{1,0:T(8,128)} custom-call(f32[4,16,128]{2,1,0:T(8,128)S(1)} %all_to_all.22.refs_0_, f32[16,32]{1,0:T(8,128)S(1)} %copy-done.4), custom_call_target="tpu_custom_call" | custom-call | tf_op jit(solution)/shard_map/pallas_call | solution.py:221
  (1 shorter events, 0.0 us)
Async XLA Ops:
  0.0 0.7 %copy-start.5 = (s32[2,1,1,16]{3,2,1,0:T(1,128)S(1)}, s32[2,1,1,16]{3,2,1,0:T(1,128)}, u32[]{:S(2)}) copy-start(s32[2,1,1,16]{3,2,1,0:T(1,128)} %param.13) | copy-start | bytes 388
  0.7 0.7 %copy-start.2 = (f32[2,1,1,16,32]{4,3,2,1,0:T(8,128)S(1)}, f32[2,1,1,16,32]{4,3,2,1,0:T(8,128)}, u32[]{:S(2)}) copy-start(f32[2,1,1,16,32]{4,3,2,1,0:T(8,128)} %param.11) | copy-start | bytes 12292
  1.4 0.7 %copy-start.3 = (f32[2,1,1,16,32]{4,3,2,1,0:T(8,128)S(1)}, f32[2,1,1,16,32]{4,3,2,1,0:T(8,128)}, u32[]{:S(2)}) copy-start(f32[2,1,1,16,32]{4,3,2,1,0:T(8,128)} %param.12) | copy-start | bytes 12292
  2.9 10.6 %copy-start.4 = (f32[16,32]{1,0:T(8,128)S(1)}, f32[16,32]{1,0:T(8,128)}, u32[]{:S(2)}) copy-start(f32[16,32]{1,0:T(8,128)} %refs_1_.3) | copy-start | bytes 6148
  2.9 18.1 %all-to-all-start = ((f32[16,1,128]{2,1,0:T(1,128)}), f32[16,1,128]{2,1,0:T(1,128)S(1)}, u32[]{:S(2)}, u32[]{:S(2)}) async-start(f32[16,1,128]{2,1,0:T(1,128)} %bitcast.6), calls=%async_computation | async-start | bytes 16384 | tf_op jit(solution)/shard_map/all_to_all | solution.py:186
  13.4 1.0 %copy-start = (bf16[2,16,8192]{2,1,0:T(8,128)(2,1)S(1)}, bf16[2,16,8192]{2,1,0:T(8,128)(2,1)}, u32[]{:S(2)}) copy-start(bf16[2,16,8192]{2,1,0:T(8,128)(2,1)} %ens_ref.1) | copy-start | bytes 1572868
  14.5 0.9 %copy-start.6 = (s32[2,1,16,8,32]{4,3,2,1,0:T(8,128)S(1)}, s32[2,1,16,8,32]{4,3,2,1,0:T(8,128)}, u32[]{:S(2)}) copy-start(s32[2,1,16,8,32]{4,3,2,1,0:T(8,128)} %param.9) | copy-start | bytes 98308
  15.4 0.9 %copy-start.7 = (s32[2,1,16,8,32]{4,3,2,1,0:T(8,128)S(1)}, s32[2,1,16,8,32]{4,3,2,1,0:T(8,128)}, u32[]{:S(2)}) copy-start(s32[2,1,16,8,32]{4,3,2,1,0:T(8,128)} %param.10) | copy-start | bytes 98308
  18.4 22.7 %copy-start.1 = (bf16[2,16,8192]{2,1,0:T(8,128)(2,1)S(1)}, bf16[2,16,8192]{2,1,0:T(8,128)(2,1)}, u32[]{:S(2)}) copy-start(bf16[2,16,8192]{2,1,0:T(8,128)(2,1)} %ens_ref.1) | copy-start | bytes 1572868

commit v2 on v1

v2 whole, which is shorter than its diff:
```python
import math

import jax
import jax.numpy as jnp
from jax import lax
from jax.experimental import pallas as pl
from jax.experimental.pallas import tpu as pltpu
from jax.sharding import PartitionSpec as P

BLOCK = 256
VMEM = pl.BlockSpec(memory_space=pltpu.VMEM)
HBM = pl.BlockSpec(memory_space=pltpu.HBM)
PARAMS = pltpu.CompilerParams(vmem_limit_bytes=32 * 1024 * 1024)
F32, BF16 = jnp.float32, jnp.bfloat16
NT = (((1,), (1,)), ((), ()))


def owned_kernel(
    innov_hbm, var_hbm, count_hbm, fb_hbm, fo_hbm, w_hbm, ens_hbm,
    out_ref, fb_ref, fo_ref, w_ref, ens_ref, innov_ref, var_ref, count_ref, sems,
):
    pairs = (
        (count_hbm, count_ref),
        (var_hbm, var_ref),
        (innov_hbm, innov_ref),
        (fo_hbm, fo_ref),
        (fb_hbm, fb_ref),
        (w_hbm, w_ref),
        (ens_hbm, ens_ref),
    )
    copies = [pltpu.make_async_copy(src, dst, sems.at[i]) for i, (src, dst) in enumerate(pairs)]
    for copy in copies:
        copy.start()
    slots, tiles, cap = innov_ref.shape
    diag = lax.broadcasted_iota(jnp.int32, (tiles, tiles), 0) == lax.broadcasted_iota(
        jnp.int32, (tiles, tiles), 1
    )
    lane = lax.broadcasted_iota(jnp.int32, (tiles, cap), 1).astype(F32)
    copies[0].wait()
    columns = []
    for t in range(slots):
        row = count_ref[t : t + 1, :].astype(F32)
        columns.append(jnp.sum(jnp.where(diag, row, 0.0), axis=1, keepdims=True))
    copies[1].wait()
    copies[2].wait()
    out_ref[...] = jnp.concatenate(
        [jnp.where(lane < columns[t], var_ref[t], 0.0) for t in range(slots)]
        + [innov_ref[t] for t in range(slots)],
        axis=1,
    )
    for copy in copies[3:]:
        copy.wait()


def pick_kernel(scale, ens_ref, w_ref, fb_ref, fo_ref, pick_ref, offr, mask_ref, fbr, field, split):
    slots, members, cells = ens_ref.shape
    blocks = cells // BLOCK
    tiles, groups, cap = fb_ref.shape[1:]
    quarters = 128 // cap
    a_rows = tiles // quarters
    for t in range(slots):
        for a in range(tiles):
            rows = pl.ds((t * a_rows + a % a_rows) * groups, groups)
            lanes = slice((a // a_rows) * cap, (a // a_rows + 1) * cap)
            fbr[rows, lanes] = fb_ref[t, a]
            offr[rows, lanes] = fo_ref[t, a]
    w = w_ref[...].astype(BF16).astype(F32)
    for b in range(blocks):
        column = w[:, b : b + 1]
        for t in range(slots):
            e = ens_ref[t, :, b * BLOCK : (b + 1) * BLOCK].astype(F32)
            field[t, b : b + 1, :] = jnp.sum(e * column, axis=0, keepdims=True)
    for t in range(slots):
        f = field[t] * scale
        upper = f.astype(BF16)
        split[t, :blocks, :] = upper
        split[t, blocks:, :] = (f - upper.astype(F32)).astype(BF16)
    off_iota = lax.broadcasted_iota(jnp.int32, (BLOCK, 128), 0)
    blk_iota = lax.broadcasted_iota(jnp.int32, (blocks, 128), 0)

    @pl.loop(0, slots * a_rows)
    def _(step):
        base = pl.multiple_of(step * groups, groups)
        off = offr[pl.ds(base, groups), :]
        blk = fbr[pl.ds(base, groups), :]
        lhs = split[step // a_rows]
        hot = jnp.concatenate(
            [(off_iota == off[r : r + 1]).astype(F32).astype(BF16) for r in range(groups)], axis=1
        )
        proj = jnp.dot(lhs, hot, preferred_element_type=F32)
        value = proj[:blocks] + proj[blocks:]
        own = jnp.concatenate(
            [(blk_iota == blk[r : r + 1]).astype(F32) for r in range(groups)], axis=1
        )
        mask_ref[step] = own.astype(BF16)
        picked = jnp.sum(own * value, axis=0, keepdims=True)
        pick_ref[pl.ds(base, groups), :] = jnp.concatenate(
            [picked[:, r * 128 : (r + 1) * 128] for r in range(groups)], axis=0
        )


def join_kernel(pick_ref, owned_ref, out_ref):
    rows = pick_ref.shape[0]
    for peer in range(out_ref.shape[0]):
        out_ref[peer, :rows, :] = pick_ref[...]
        out_ref[peer, rows:, :] = owned_ref[...]


def gradient_kernel(ens_ref, got_ref, off_ref, mask_ref, out_ref, res):
    slots, members, cells = ens_ref.shape
    blocks = cells // BLOCK
    groups = got_ref.shape[0]
    a_rows = mask_ref.shape[0] // slots
    rows = slots * a_rows * groups
    tiles = got_ref.shape[1] - rows
    quarters = tiles // a_rows
    cap = 128 // quarters
    quarter = lax.broadcasted_iota(jnp.int32, (groups, 128), 1) // cap

    def aligned(message, source, target):
        shift = (target - source) * cap % 128
        return pltpu.roll(message, shift, 1) if shift else message

    for a in range(a_rows):
        messages = [got_ref[:, rows + a + q * a_rows, :] for q in range(quarters)]
        for t in range(slots):
            w = jnp.zeros((groups, 128), F32)
            i = jnp.zeros((groups, 128), F32)
            for q in range(quarters):
                w = jnp.where(quarter == q, aligned(messages[q], t, q), w)
                i = jnp.where(quarter == q, aligned(messages[q], slots + t, q), i)
            at = pl.ds((t * a_rows + a) * groups, groups)
            x = got_ref[0, at, :]
            for peer in range(1, groups):
                x = x + got_ref[peer, at, :]
            res[at, :] = w * (x - i)
    off_iota = lax.broadcasted_iota(jnp.int32, (BLOCK, 128), 0)
    local = None
    for t in range(slots):
        total = jnp.zeros((2 * blocks, BLOCK), F32)
        for step in range(t * a_rows, (t + 1) * a_rows):
            value = res[step * groups : (step + 1) * groups, :]
            upper = value.astype(BF16)
            lower = (value - upper.astype(F32)).astype(BF16)
            own = mask_ref[step]
            both = jnp.concatenate(
                [
                    jnp.concatenate(
                        [own[:, r * 128 : (r + 1) * 128] * part[r : r + 1] for r in range(groups)],
                        axis=1,
                    )
                    for part in (upper, lower)
                ],
                axis=0,
            )
            off = off_ref[step * groups : (step + 1) * groups, :]
            hot = jnp.concatenate(
                [(off_iota == off[r : r + 1]).astype(F32).astype(BF16) for r in range(groups)],
                axis=1,
            )
            total += lax.dot_general(both, hot, NT, preferred_element_type=F32)
        adjoint = (total[:blocks] + total[blocks:]).astype(BF16)
        lhs = jnp.concatenate(
            [ens_ref[t, :, b * BLOCK : (b + 1) * BLOCK] for b in range(blocks)], axis=0
        )
        prod = lax.dot_general(lhs, adjoint, NT, preferred_element_type=F32)
        part = prod.reshape(blocks, members, blocks)
        own = lax.broadcasted_iota(jnp.int32, part.shape, 0) == lax.broadcasted_iota(
            jnp.int32, part.shape, 2
        )
        part = jnp.sum(jnp.where(own, part, 0.0), axis=0)
        local = part if local is None else local + part
    padded = jnp.concatenate([local, jnp.zeros((members, 128 - blocks), F32)], axis=1)
    for peer in range(out_ref.shape[0]):
        out_ref[peer] = padded


def finish_kernel(scale, got_ref, w_ref, out_ref):
    total = got_ref[0]
    for peer in range(1, got_ref.shape[0]):
        total = total + got_ref[peer]
    out_ref[...] = w_ref[...] + scale * total[:, : w_ref.shape[1]]


def cost(flops, read):
    return pl.CostEstimate(flops=flops, bytes_accessed=read, transcendentals=0)


def in_hbm(array):
    return pltpu.with_memory_space_constraint(array, pltpu.HBM)


def in_vmem(shape, dtype):
    return pltpu.VMEM(shape, dtype)


def shards(ens_pert, weights, foot_block, foot_offset, innovation, inv_var, obs_count):
    groups = lax.axis_size("member")
    windows = lax.axis_size("tm")
    slots, members, cells = ens_pert.shape
    blocks = cells // BLOCK
    tiles, _, cap = foot_block.shape[2:]
    rows = slots * tiles * groups * cap // 128
    steps = rows // groups
    scale = 1.0 / math.sqrt(members * groups - 1)
    owned, fb, fo, w, ens = pl.pallas_call(
        owned_kernel,
        out_shape=(
            jax.ShapeDtypeStruct((tiles, 128), F32),
            in_vmem((slots, tiles, groups, cap), jnp.int32),
            in_vmem((slots, tiles, groups, cap), jnp.int32),
            in_vmem(weights.shape, F32),
            in_vmem(ens_pert.shape, BF16),
        ),
        in_specs=[HBM] * 7,
        out_specs=(VMEM,) * 5,
        scratch_shapes=[
            pltpu.VMEM((slots, tiles, cap), F32),
            pltpu.VMEM((slots, tiles, cap), F32),
            pltpu.VMEM((slots, tiles), jnp.int32),
            pltpu.SemaphoreType.DMA((7,)),
        ],
        compiler_params=PARAMS,
    )(
        in_hbm(innovation.reshape(slots, tiles, cap)),
        in_hbm(inv_var.reshape(slots, tiles, cap)),
        in_hbm(obs_count.reshape(slots, tiles)),
        in_hbm(foot_block.reshape(slots, tiles, groups, cap)),
        in_hbm(foot_offset.reshape(slots, tiles, groups, cap)),
        in_hbm(weights),
        in_hbm(ens_pert),
    )
    owned = lax.all_to_all(owned, "space", 0, 0, tiled=True)
    picks, offsets, mask = pl.pallas_call(
        lambda *refs: pick_kernel(scale, *refs),
        out_shape=(
            in_vmem((rows, 128), F32),
            in_vmem((rows, 128), jnp.int32),
            in_vmem((steps, blocks, groups * 128), BF16),
        ),
        in_specs=[VMEM] * 4,
        out_specs=(VMEM,) * 3,
        scratch_shapes=[
            pltpu.VMEM((rows, 128), jnp.int32),
            pltpu.VMEM((slots, blocks, BLOCK), F32),
            pltpu.VMEM((slots, 2 * blocks, BLOCK), BF16),
        ],
        compiler_params=PARAMS,
        cost_estimate=cost(4 * blocks * rows * 128 * BLOCK, 2 << 20),
    )(ens, w, fb, fo)
    joined = pl.pallas_call(
        join_kernel,
        out_shape=jax.ShapeDtypeStruct((groups, rows + tiles, 128), F32),
        in_specs=[VMEM] * 2,
        out_specs=VMEM,
        compiler_params=PARAMS,
    )(picks, owned)
    got = lax.all_to_all(joined, "member", 0, 0, tiled=True)
    local = pl.pallas_call(
        gradient_kernel,
        out_shape=jax.ShapeDtypeStruct((windows, members, 128), F32),
        in_specs=[VMEM] * 4,
        out_specs=VMEM,
        scratch_shapes=[pltpu.VMEM((rows, 128), F32)],
        compiler_params=PARAMS,
    )(ens, got, offsets, mask)
    parts = lax.all_to_all(local, "tm", 0, 0, tiled=True)
    return pl.pallas_call(
        lambda *refs: finish_kernel(scale, *refs),
        out_shape=jax.ShapeDtypeStruct(weights.shape, F32),
        in_specs=[VMEM] * 2,
        out_specs=VMEM,
        compiler_params=PARAMS,
    )(parts, w)


def solution(mesh):
    in_specs = (
        P("tm", "member", "space"),
        P("member", "space"),
        P("tm", "space", None, None, None),
        P("tm", "space", None, None, None),
        P("tm", "space", "member", None, None),
        P("tm", "space", "member", None, None),
        P("tm", "space", "member", None),
    )
    out_specs = P("member", "space")
    return jax.shard_map(shards, mesh=mesh, in_specs=in_specs, out_specs=out_specs, check_vma=False)
```

time: 53.7 us -> 52.3 us (0.974)
  local copies, waits for them, and re-layouts: 4.97 us -> 0 us
  waiting for transfers between devices: 2.47 us -> 5.36 us
  Pallas kernels: 6.44 us -> 7.46 us
    unnamed x16 -> x0, local copies, waits for them, and re-layouts: 4.97 us -> none
    all_to_all x1, waiting for transfers between devices: 2.47 us -> 5.36 us  [shards(): owned = lax.all_to_all(owned, 'space', 0, 0, tiled=True)]
    pallas_call x2, Pallas kernels: 2.89 us -> 4.02 us  [the longest x1 2.13 us: shards(): pl.pallas_call(lambda *refs: pick_kernel(scale, *refs), out_shape=(in_vme...]
where the time goes in v2:
time: 52.3 us; the launch traced here: 52.1 us
  blocking collectives  28.8 us (55%)
  starting transfers between devices  10.4 us (20%)
  Pallas kernels  7.46 us (14%)
  waiting for transfers between devices  5.36 us (10%)
    all_to_all x1, blocking collectives, shards(): got = lax.all_to_all(joined, 'member', 0, 0, tiled=True)  20.2 us
    all_to_all x1, starting transfers between devices, shards(): owned = lax.all_to_all(owned, 'space', 0, 0, tiled=True)  10.4 us
    all_to_all x1, blocking collectives, shards(): parts = lax.all_to_all(local, 'tm', 0, 0, tiled=True)  8.62 us
    all_to_all x1, waiting for transfers between devices, shards(): owned = lax.all_to_all(owned, 'space', 0, 0, tiled=True)  5.36 us
    pallas_call x1, Pallas kernels, shards(): pl.pallas_call(gradient_kernel, out_shape=jax.ShapeDtypeStruct((windows,...  2.81 us
    pallas_call x1, Pallas kernels, shards(): pl.pallas_call(lambda *refs: pick_kernel(scale, *refs), out_shape=(in_vme...  2.13 us
    pallas_call x1, Pallas kernels, shards(): pl.pallas_call(owned_kernel, out_shape=(jax.ShapeDtypeStruct((tiles, 128)...  1.89 us
  transfers between devices with their start and end apart: 1, of which 1 were waited for; matrix products, arithmetic and copies ran while one was open for 0% of the time, Pallas kernels for 4%

profile of v2, /device:TPU:2, one launch (start us, length us, event | category | flops | bytes accessed | tf_op | source)
XLA Modules:
  0.0 52.1 jit_solution(5761024330009006518)
XLA Ops:
  0.0 1.9 %shard_map.73 = (f32[16,128]{1,0:T(8,128)}, s32[2,16,8,32]{3,2,1,0:T(8,128)S(1)}, s32[2,16,8,32]{3,2,1,0:T(8,128)S(1)}, f32[16,32]{1,0:T(8,128)S(1)}, bf16[2,16,8192]{2,1,0:T(8,128)(2,1)S(1)}) custom-call(f32[2,16,32]{2,1,0:T(8,128)} %bitcast.12, f32[2,16,32]{2,1,0:T(8,128)} %bitcast.13, s32[2,16]{1,0:T(2,128)} %bitcast.14, s32[2,16,8,32]{3,2,1,0:T(8,128)} %bitcast.10, ...), custom_call_target="tpu_custom_call" | custom-call | tf_op jit(solution)/shard_map/pallas_call | solution.py:206
  1.9 10.4 %all-to-all-start = ((f32[16,1,128]{2,1,0:T(1,128)}), f32[16,1,128]{2,1,0:T(1,128)S(1)}, u32[]{:S(2)}, u32[]{:S(2)}) async-start(f32[16,1,128]{2,1,0:T(1,128)} %bitcast.6), calls=%async_computation | async-start | bytes 16384 | tf_op jit(solution)/shard_map/all_to_all | solution.py:233
  12.3 2.1 %shard_map.74 = (f32[64,128]{1,0:T(8,128)S(1)}, s32[64,128]{1,0:T(8,128)S(1)}, bf16[8,32,1024]{2,1,0:T(8,128)(2,1)S(1)}) custom-call(bf16[2,16,8192]{2,1,0:T(8,128)(2,1)S(1)} %get-tuple-element.13.refs_0_.ens_ref, f32[16,32]{1,0:T(8,128)S(1)} %get-tuple-element.14.refs_1_, s32[2,16,8,32]{3,2,1,0:T(8,128)S(1)} %get-tuple-element.15.refs_2_, ...), custom_call_target="tpu_custom_call" | custom-call | flops 268435456 | bytes 2097152 | tf_op jit(solution)/shard_map/pallas_call | solution.py:234
  14.5 5.4 %all-to-all-done = f32[16,1,128]{2,1,0:T(1,128)S(1)} async-done(((f32[16,1,128]{2,1,0:T(1,128)}), f32[16,1,128]{2,1,0:T(1,128)S(1)}, u32[]{:S(2)}, u32[]{:S(2)}) %all-to-all-start) | async-done | bytes 8224 | tf_op jit(solution)/shard_map/all_to_all | solution.py:233
  19.9 20.2 %all_to_all.21.got_ref = f32[8,80,128]{2,1,0:T(8,128)S(1)} all-to-all(f32[8,80,128]{2,1,0:T(8,128)S(1)} %shard_map.75), channel_id=1, replica_groups=mesh['space'=16,'member'=8,'tm'=4] {'member'}, dimensions={0} | all-to-all | bytes 655360 | tf_op jit(solution)/shard_map/all_to_all | solution.py:258
  40.1 2.8 %shard_map.76 = f32[4,16,128]{2,1,0:T(8,128)S(1)} custom-call(bf16[2,16,8192]{2,1,0:T(8,128)(2,1)S(1)} %get-tuple-element.13.refs_0_.ens_ref, f32[8,80,128]{2,1,0:T(8,128)S(1)} %all_to_all.21.got_ref, s32[64,128]{1,0:T(8,128)S(1)} %get-tuple-element.19.off_ref, bf16[8,32,1024]{2,1,0:T(8,128)(2,1)S(1)} %get-tuple-element.20.mask_ref), custom_call_target="tpu_custom_call" | custom-call | tf_op jit(solution)/shard_map/pallas_call | solution.py:259
  42.9 8.6 %all_to_all.22.refs_0_ = f32[4,16,128]{2,1,0:T(8,128)S(1)} all-to-all(f32[4,16,128]{2,1,0:T(8,128)S(1)} %shard_map.76), channel_id=1, replica_groups=mesh['space'=16,'member'=8,'tm'=4] {'tm'}, dimensions={0} | all-to-all | bytes 65536 | tf_op jit(solution)/shard_map/all_to_all | solution.py:267
  51.5 0.6 %shard_map.77 = f32[16,32]{1,0:T(8,128)} custom-call(f32[4,16,128]{2,1,0:T(8,128)S(1)} %all_to_all.22.refs_0_, f32[16,32]{1,0:T(8,128)S(1)} %get-tuple-element.14.refs_1_), custom_call_target="tpu_custom_call" | custom-call | tf_op jit(solution)/shard_map/pallas_call | solution.py:268
  (1 shorter events, 0.0 us)
Async XLA Ops:
  1.9 17.9 %all-to-all-start = ((f32[16,1,128]{2,1,0:T(1,128)}), f32[16,1,128]{2,1,0:T(1,128)S(1)}, u32[]{:S(2)}, u32[]{:S(2)}) async-start(f32[16,1,128]{2,1,0:T(1,128)} %bitcast.6), calls=%async_computation | async-start | bytes 16384 | tf_op jit(solution)/shard_map/all_to_all | solution.py:233

commit v3 on v2

v3 whole, which is shorter than its diff:
```python
import math

import jax
import jax.numpy as jnp
from jax import lax
from jax.experimental import pallas as pl
from jax.experimental.pallas import tpu as pltpu
from jax.sharding import PartitionSpec as P

BLOCK = 256
LANES = 128
VMEM = pl.BlockSpec(memory_space=pltpu.VMEM)
HBM = pl.BlockSpec(memory_space=pltpu.HBM)
PARAMS = pltpu.CompilerParams(vmem_limit_bytes=32 * 1024 * 1024)
F32, BF16 = jnp.float32, jnp.bfloat16
NT = (((1,), (1,)), ((), ()))


def fetch(sems, *pairs):
    copies = [pltpu.make_async_copy(src, dst, sems.at[i]) for i, (src, dst) in enumerate(pairs)]
    for copy in copies:
        copy.start()
    return copies


def owned_kernel(innov_hbm, var_hbm, count_hbm, out_ref, innov_ref, var_ref, count_ref, sems):
    copies = fetch(sems, (count_hbm, count_ref), (var_hbm, var_ref), (innov_hbm, innov_ref))
    slots, tiles, cap = innov_ref.shape
    diag = lax.broadcasted_iota(jnp.int32, (tiles, tiles), 0) == lax.broadcasted_iota(
        jnp.int32, (tiles, tiles), 1
    )
    lane = lax.broadcasted_iota(jnp.int32, (tiles, cap), 1).astype(F32)
    copies[0].wait()
    columns = []
    for t in range(slots):
        row = count_ref[t : t + 1, :].astype(F32)
        columns.append(jnp.sum(jnp.where(diag, row, 0.0), axis=1, keepdims=True))
    copies[1].wait()
    copies[2].wait()
    out_ref[...] = jnp.concatenate(
        [jnp.where(lane < columns[t], var_ref[t], 0.0) for t in range(slots)]
        + [innov_ref[t] for t in range(slots)],
        axis=1,
    )


def hot_rows(ids, count):
    iota = lax.broadcasted_iota(jnp.int32, (count, LANES), 0)
    return jnp.concatenate(
        [(iota == ids[r : r + 1]).astype(F32) for r in range(ids.shape[0])], axis=1
    )


def pick_kernel(
    scale, ens_hbm, w_hbm, fb_hbm, fo_hbm, pick_ref, hot_ref, high_ref,
    ens_ref, w_ref, fb_ref, fo_ref, low, field, split, sems,
):
    copies = fetch(sems, (fo_hbm, fo_ref), (fb_hbm, fb_ref), (w_hbm, w_ref), (ens_hbm, ens_ref))
    slots, members, cells = ens_ref.shape
    blocks = cells // BLOCK
    highs = cells // LANES
    tiles, groups, cap = fb_ref.shape[1:]
    quarters = LANES // cap
    a_rows = tiles // quarters
    copies[0].wait()
    copies[1].wait()
    for t in range(slots):
        for a in range(tiles):
            rows = pl.ds((t * a_rows + a % a_rows) * groups, groups)
            lanes = slice((a // a_rows) * cap, (a // a_rows + 1) * cap)
            offset = fo_ref[t, a]
            upper_half = offset >= LANES
            high_ref[rows, lanes] = fb_ref[t, a] + jnp.where(upper_half, blocks, 0)
            low[rows, lanes] = jnp.where(upper_half, offset - LANES, offset)
    copies[2].wait()
    copies[3].wait()
    w = w_ref[...].astype(BF16).astype(F32)
    for b in range(blocks):
        column = w[:, b : b + 1]
        for t in range(slots):
            e = ens_ref[t, :, b * BLOCK : (b + 1) * BLOCK].astype(F32)
            sums = jnp.sum(e * column, axis=0, keepdims=True)
            field[t, b : b + 1, :] = sums[:, :LANES]
            field[t, blocks + b : blocks + b + 1, :] = sums[:, LANES:]
    for t in range(slots):
        f = field[t] * scale
        upper = f.astype(BF16)
        split[t, :highs, :] = upper
        split[t, highs:, :] = (f - upper.astype(F32)).astype(BF16)

    @pl.loop(0, slots * a_rows)
    def _(step):
        base = pl.multiple_of(step * groups, groups)
        hot = hot_rows(low[pl.ds(base, groups), :], LANES).astype(BF16)
        hot_ref[step] = hot.T
        proj = jnp.dot(split[step // a_rows], hot, preferred_element_type=F32)
        own = hot_rows(high_ref[pl.ds(base, groups), :], highs)
        picked = jnp.sum(own * (proj[:highs] + proj[highs:]), axis=0, keepdims=True)
        pick_ref[pl.ds(base, groups), :] = jnp.concatenate(
            [picked[:, r * LANES : (r + 1) * LANES] for r in range(groups)], axis=0
        )


def join_kernel(pick_ref, owned_ref, out_ref):
    groups = out_ref.shape[0]
    rows = pick_ref.shape[0]
    tiles = owned_ref.shape[0]
    a_rows = (out_ref.shape[1] - rows) // 2
    quarters = tiles // a_rows
    cap = LANES // quarters
    slots = rows // (a_rows * groups)
    quarter = lax.broadcasted_iota(jnp.int32, (a_rows, LANES), 1) // cap
    sublane = lax.broadcasted_iota(jnp.int32, (groups, LANES), 0)
    own_group = sublane == lax.axis_index("member")

    def aligned(source):
        total = None
        for q in range(quarters):
            part = owned_ref[q * a_rows : (q + 1) * a_rows, :]
            shift = (q - source) * cap % LANES
            part = pltpu.roll(part, shift, 1) if shift else part
            total = part if total is None else jnp.where(quarter == q, part, total)
        return total

    weights = jnp.concatenate([aligned(t) for t in range(slots)], axis=0)
    for t in range(slots):
        innov = aligned(slots + t)
        for a in range(a_rows):
            at = slice((t * a_rows + a) * groups, (t * a_rows + a + 1) * groups)
            value = pick_ref[at, :] - jnp.where(own_group, innov[a : a + 1], 0.0)
            for peer in range(groups):
                out_ref[peer, at, :] = value
    for peer in range(groups):
        out_ref[peer, rows:, :] = weights


def gradient_kernel(ens_ref, got_ref, hot_ref, high_ref, out_ref):
    slots, members, cells = ens_ref.shape
    blocks = cells // BLOCK
    highs = cells // LANES
    groups = got_ref.shape[0]
    rows = high_ref.shape[0]
    a_rows = rows // (slots * groups)
    local = None
    for t in range(slots):
        total = jnp.zeros((2 * highs, LANES), F32)
        for step in range(t * a_rows, (t + 1) * a_rows):
            at = slice(step * groups, (step + 1) * groups)
            value = got_ref[0, at, :]
            for peer in range(1, groups):
                value = value + got_ref[peer, at, :]
            value = value * got_ref[:, rows + step, :]
            upper = value.astype(BF16)
            lower = (value - upper.astype(F32)).astype(BF16)
            own = hot_rows(high_ref[at, :], highs).astype(BF16)
            both = jnp.concatenate(
                [
                    jnp.concatenate(
                        [
                            own[:, r * LANES : (r + 1) * LANES] * part[r : r + 1]
                            for r in range(groups)
                        ],
                        axis=1,
                    )
                    for part in (upper, lower)
                ],
                axis=0,
            )
            total += jnp.dot(both, hot_ref[step], preferred_element_type=F32)
        adjoint = (total[:highs] + total[highs:]).astype(BF16)
        adjoint = jnp.concatenate([adjoint[:blocks], adjoint[blocks:]], axis=1)
        lhs = jnp.concatenate(
            [ens_ref[t, :, b * BLOCK : (b + 1) * BLOCK] for b in range(blocks)], axis=0
        )
        prod = lax.dot_general(lhs, adjoint, NT, preferred_element_type=F32)
        part = prod.reshape(blocks, members, blocks)
        own = lax.broadcasted_iota(jnp.int32, part.shape, 0) == lax.broadcasted_iota(
            jnp.int32, part.shape, 2
        )
        part = jnp.sum(jnp.where(own, part, 0.0), axis=0)
        local = part if local is None else local + part
    height = out_ref.shape[1]
    dense = jnp.concatenate(
        [local[r : r + height] for r in range(0, members, height)], axis=1
    )
    for peer in range(out_ref.shape[0]):
        out_ref[peer] = dense


def finish_kernel(scale, got_ref, w_ref, out_ref):
    total = got_ref[0]
    for peer in range(1, got_ref.shape[0]):
        total = total + got_ref[peer]
    blocks = w_ref.shape[1]
    total = jnp.concatenate(
        [total[:, c : c + blocks] for c in range(0, LANES, blocks)], axis=0
    )
    out_ref[...] = w_ref[...] + scale * total


def cost(flops, read):
    return pl.CostEstimate(flops=flops, bytes_accessed=read, transcendentals=0)


def in_hbm(array):
    return pltpu.with_memory_space_constraint(array, pltpu.HBM)


def in_vmem(shape, dtype):
    return pltpu.VMEM(shape, dtype)


def shards(ens_pert, weights, foot_block, foot_offset, innovation, inv_var, obs_count):
    groups = lax.axis_size("member")
    windows = lax.axis_size("tm")
    slots, members, cells = ens_pert.shape
    blocks = cells // BLOCK
    highs = cells // LANES
    tiles, _, cap = foot_block.shape[2:]
    rows = slots * tiles * groups * cap // LANES
    steps = rows // groups
    scale = 1.0 / math.sqrt(members * groups - 1)
    owned = pl.pallas_call(
        owned_kernel,
        out_shape=jax.ShapeDtypeStruct((tiles, LANES), F32),
        in_specs=[HBM] * 3,
        out_specs=VMEM,
        scratch_shapes=[
            pltpu.VMEM((slots, tiles, cap), F32),
            pltpu.VMEM((slots, tiles, cap), F32),
            pltpu.VMEM((slots, tiles), jnp.int32),
            pltpu.SemaphoreType.DMA((3,)),
        ],
        compiler_params=PARAMS,
    )(
        in_hbm(innovation.reshape(slots, tiles, cap)),
        in_hbm(inv_var.reshape(slots, tiles, cap)),
        in_hbm(obs_count.reshape(slots, tiles)),
    )
    owned = lax.all_to_all(owned, "space", 0, 0, tiled=True)
    picks, hot, high = pl.pallas_call(
        lambda *refs: pick_kernel(scale, *refs),
        out_shape=(
            in_vmem((rows, LANES), F32),
            in_vmem((steps, groups * LANES, LANES), BF16),
            in_vmem((rows, LANES), jnp.int32),
        ),
        in_specs=[HBM] * 4,
        out_specs=(VMEM,) * 3,
        scratch_shapes=[
            pltpu.VMEM(ens_pert.shape, BF16),
            pltpu.VMEM(weights.shape, F32),
            pltpu.VMEM((slots, tiles, groups, cap), jnp.int32),
            pltpu.VMEM((slots, tiles, groups, cap), jnp.int32),
            pltpu.VMEM((rows, LANES), jnp.int32),
            pltpu.VMEM((slots, highs, LANES), F32),
            pltpu.VMEM((slots, 2 * highs, LANES), BF16),
            pltpu.SemaphoreType.DMA((4,)),
        ],
        compiler_params=PARAMS,
        cost_estimate=cost(4 * blocks * rows * LANES * BLOCK, 4 << 20),
    )(
        in_hbm(ens_pert),
        in_hbm(weights),
        in_hbm(foot_block.reshape(slots, tiles, groups, cap)),
        in_hbm(foot_offset.reshape(slots, tiles, groups, cap)),
    )
    joined = pl.pallas_call(
        join_kernel,
        out_shape=jax.ShapeDtypeStruct((groups, rows + steps, LANES), F32),
        in_specs=[VMEM] * 2,
        out_specs=VMEM,
        compiler_params=PARAMS,
    )(picks, owned)
    got = lax.all_to_all(joined, "member", 0, 0, tiled=True)
    local = pl.pallas_call(
        gradient_kernel,
        out_shape=jax.ShapeDtypeStruct((windows, members * blocks // LANES, LANES), F32),
        in_specs=[VMEM] * 4,
        out_specs=VMEM,
        compiler_params=PARAMS,
    )(ens_pert, got, hot, high)
    parts = lax.all_to_all(local, "tm", 0, 0, tiled=True)
    return pl.pallas_call(
        lambda *refs: finish_kernel(scale, *refs),
        out_shape=jax.ShapeDtypeStruct(weights.shape, F32),
        in_specs=[VMEM] * 2,
        out_specs=VMEM,
        compiler_params=PARAMS,
    )(parts, weights)


def solution(mesh):
    in_specs = (
        P("tm", "member", "space"),
        P("member", "space"),
        P("tm", "space", None, None, None),
        P("tm", "space", None, None, None),
        P("tm", "space", "member", None, None),
        P("tm", "space", "member", None, None),
        P("tm", "space", "member", None),
    )
    out_specs = P("member", "space")
    return jax.shard_map(shards, mesh=mesh, in_specs=in_specs, out_specs=out_specs, check_vma=False)
```

time: 52.3 us -> 49.8 us (0.952)
  waiting for transfers between devices: 5.36 us -> 3.8 us
  blocking collectives: 28.8 us -> 28 us
    all_to_all x1, waiting for transfers between devices: 5.36 us -> 3.8 us  [shards(): owned = lax.all_to_all(owned, 'space', 0, 0, tiled=True)]
    pallas_call x1, Pallas kernels: 2.13 us -> 3.68 us  [shards(): pl.pallas_call(lambda *refs: pick_kernel(scale, *refs), out_shape=(in_vme...]
    pallas_call x1, Pallas kernels: 2.81 us -> 1.31 us  [shards(): pl.pallas_call(gradient_kernel, out_shape=jax.ShapeDtypeStruct((windows,...]
    all_to_all x1, blocking collectives: 20.2 us -> 19.5 us  [shards(): got = lax.all_to_all(joined, 'member', 0, 0, tiled=True)]
  transfers between devices with their start and end apart: 1 -> 1, of which waited for: 1 -> 1; matrix products, arithmetic and copies ran while one was open for 0% -> 0% of each run, Pallas kernels for 4% -> 7%
where the time goes in v3:
time: 49.8 us; the launch traced here: 49.5 us
  blocking collectives  28 us (56%)
  starting transfers between devices  10.4 us (21%)
  Pallas kernels  7.27 us (15%)
  waiting for transfers between devices  3.8 us (8%)
    all_to_all x1, blocking collectives, shards(): got = lax.all_to_all(joined, 'member', 0, 0, tiled=True)  19.5 us
    all_to_all x1, starting transfers between devices, shards(): owned = lax.all_to_all(owned, 'space', 0, 0, tiled=True)  10.4 us
    all_to_all x1, blocking collectives, shards(): parts = lax.all_to_all(local, 'tm', 0, 0, tiled=True)  8.48 us
    all_to_all x1, waiting for transfers between devices, shards(): owned = lax.all_to_all(owned, 'space', 0, 0, tiled=True)  3.8 us
    pallas_call x1, Pallas kernels, shards(): pl.pallas_call(lambda *refs: pick_kernel(scale, *refs), out_shape=(in_vme...  3.68 us
    pallas_call x1, Pallas kernels, shards(): pl.pallas_call(owned_kernel, out_shape=jax.ShapeDtypeStruct((tiles, LANES...  1.52 us
    pallas_call x1, Pallas kernels, shards(): pl.pallas_call(gradient_kernel, out_shape=jax.ShapeDtypeStruct((windows,...  1.31 us
  transfers between devices with their start and end apart: 1, of which 1 were waited for; matrix products, arithmetic and copies ran while one was open for 0% of the time, Pallas kernels for 7%

profile of v3, /device:TPU:2, one launch (start us, length us, event | category | flops | bytes accessed | tf_op | source)
XLA Modules:
  0.0 49.5 jit_solution(13490604508390671825)
XLA Ops:
  0.0 0.0 copy-start
  0.0 1.5 %shard_map.74 = f32[16,128]{1,0:T(8,128)} custom-call(f32[2,16,32]{2,1,0:T(8,128)} %bitcast.10, f32[2,16,32]{2,1,0:T(8,128)} %bitcast.11, s32[2,16]{1,0:T(2,128)} %bitcast.12), custom_call_target="tpu_custom_call" | custom-call | tf_op jit(solution)/shard_map/pallas_call | solution.py:223
  1.5 10.4 %all-to-all-start = ((f32[16,1,128]{2,1,0:T(1,128)}), f32[16,1,128]{2,1,0:T(1,128)S(1)}, u32[]{:S(2)}, u32[]{:S(2)}) async-start(f32[16,1,128]{2,1,0:T(1,128)} %bitcast.6), calls=%async_computation | async-start | bytes 16384 | tf_op jit(solution)/shard_map/all_to_all | solution.py:240
  12.0 3.7 %shard_map.73 = (f32[64,128]{1,0:T(8,128)S(1)}, bf16[8,1024,128]{2,1,0:T(8,128)(2,1)S(1)}, s32[64,128]{1,0:T(8,128)S(1)}) custom-call(bf16[2,16,8192]{2,1,0:T(8,128)(2,1)} %ens_ref.1, f32[16,32]{1,0:T(8,128)} %refs_1_.3, s32[2,16,8,32]{3,2,1,0:T(8,128)} %bitcast.13, s32[2,16,8,32]{3,2,1,0:T(8,128)} %bitcast.14), custom_call_target="tpu_custom_call" | custom-call | flops 268435456 | bytes 4194304 | tf_op jit(solution)/shard_map/pallas_call | solution.py:241
  15.7 0.0 copy-start.1
  15.7 3.8 %all-to-all-done = f32[16,1,128]{2,1,0:T(1,128)S(1)} async-done(((f32[16,1,128]{2,1,0:T(1,128)}), f32[16,1,128]{2,1,0:T(1,128)S(1)}, u32[]{:S(2)}, u32[]{:S(2)}) %all-to-all-start) | async-done | bytes 8224 | tf_op jit(solution)/shard_map/all_to_all | solution.py:240
  19.5 0.1 shard_map.75
  19.6 19.5 %all_to_all.21.got_ref = f32[8,72,128]{2,1,0:T(8,128)S(1)} all-to-all(f32[8,72,128]{2,1,0:T(8,128)S(1)} %shard_map.75), channel_id=1, replica_groups=mesh['space'=16,'member'=8,'tm'=4] {'member'}, dimensions={0} | all-to-all | bytes 589824 | tf_op jit(solution)/shard_map/all_to_all | solution.py:275
  39.1 0.0 copy-done
  39.1 1.3 %shard_map.76 = f32[4,4,128]{2,1,0:T(4,128)S(1)} custom-call(bf16[2,16,8192]{2,1,0:T(8,128)(2,1)S(1)} %copy-done, f32[8,72,128]{2,1,0:T(8,128)S(1)} %all_to_all.21.got_ref, bf16[8,1024,128]{2,1,0:T(8,128)(2,1)S(1)} %get-tuple-element.9.hot_ref, s32[64,128]{1,0:T(8,128)S(1)} %get-tuple-element.10.high_ref), custom_call_target="tpu_custom_call" | custom-call | tf_op jit(solution)/shard_map/pallas_call | solution.py:276
  40.4 8.5 %all_to_all.22.refs_0_ = f32[4,4,128]{2,1,0:T(4,128)S(1)} all-to-all(f32[4,4,128]{2,1,0:T(4,128)S(1)} %shard_map.76), channel_id=1, replica_groups=mesh['space'=16,'member'=8,'tm'=4] {'tm'}, dimensions={0} | all-to-all | bytes 16384 | tf_op jit(solution)/shard_map/all_to_all | solution.py:283
  48.9 0.0 copy-done.1
  48.9 0.7 %shard_map.77 = f32[16,32]{1,0:T(8,128)} custom-call(f32[4,4,128]{2,1,0:T(4,128)S(1)} %all_to_all.22.refs_0_, f32[16,32]{1,0:T(8,128)S(1)} %copy-done.1), custom_call_target="tpu_custom_call" | custom-call | tf_op jit(solution)/shard_map/pallas_call | solution.py:284
Async XLA Ops:
  0.0 39.1 %copy-start = (bf16[2,16,8192]{2,1,0:T(8,128)(2,1)S(1)}, bf16[2,16,8192]{2,1,0:T(8,128)(2,1)}, u32[]{:S(2)}) copy-start(bf16[2,16,8192]{2,1,0:T(8,128)(2,1)} %ens_ref.1) | copy-start | bytes 1572868
  1.5 17.9 %all-to-all-start = ((f32[16,1,128]{2,1,0:T(1,128)}), f32[16,1,128]{2,1,0:T(1,128)S(1)}, u32[]{:S(2)}, u32[]{:S(2)}) async-start(f32[16,1,128]{2,1,0:T(1,128)} %bitcast.6), calls=%async_computation | async-start | bytes 16384 | tf_op jit(solution)/shard_map/all_to_all | solution.py:240
  15.7 33.2 %copy-start.1 = (f32[16,32]{1,0:T(8,128)S(1)}, f32[16,32]{1,0:T(8,128)}, u32[]{:S(2)}) copy-start(f32[16,32]{1,0:T(8,128)} %refs_1_.3) | copy-start | bytes 6148

commit v4 on v3

--- a/solution.py
+++ b/solution.py
@@ -13,7 +13,6 @@
 HBM = pl.BlockSpec(memory_space=pltpu.HBM)
 PARAMS = pltpu.CompilerParams(vmem_limit_bytes=32 * 1024 * 1024)
 F32, BF16 = jnp.float32, jnp.bfloat16
-NT = (((1,), (1,)), ((), ()))
 
 
 def fetch(sems, *pairs):
@@ -141,7 +140,7 @@
     groups = got_ref.shape[0]
     rows = high_ref.shape[0]
     a_rows = rows // (slots * groups)
-    local = None
+    sums = [None] * blocks
     for t in range(slots):
         total = jnp.zeros((2 * highs, LANES), F32)
         for step in range(t * a_rows, (t + 1) * a_rows):
@@ -169,16 +168,12 @@
             total += jnp.dot(both, hot_ref[step], preferred_element_type=F32)
         adjoint = (total[:highs] + total[highs:]).astype(BF16)
         adjoint = jnp.concatenate([adjoint[:blocks], adjoint[blocks:]], axis=1)
-        lhs = jnp.concatenate(
-            [ens_ref[t, :, b * BLOCK : (b + 1) * BLOCK] for b in range(blocks)], axis=0
-        )
-        prod = lax.dot_general(lhs, adjoint, NT, preferred_element_type=F32)
-        part = prod.reshape(blocks, members, blocks)
-        own = lax.broadcasted_iota(jnp.int32, part.shape, 0) == lax.broadcasted_iota(
-            jnp.int32, part.shape, 2
-        )
-        part = jnp.sum(jnp.where(own, part, 0.0), axis=0)
-        local = part if local is None else local + part
+        adjoint = adjoint.astype(F32)
+        for b in range(blocks):
+            e = ens_ref[t, :, b * BLOCK : (b + 1) * BLOCK].astype(F32) * adjoint[b : b + 1]
+            e = e[:, :LANES] + e[:, LANES:]
+            sums[b] = e if t == 0 else sums[b] + e
+    local = jnp.concatenate([jnp.sum(e, axis=1, keepdims=True) for e in sums], axis=1)
     height = out_ref.shape[1]
     dense = jnp.concatenate(
         [local[r : r + height] for r in range(0, members, height)], axis=1

time: 49.8 us -> 49.5 us (level)
  no operation moved by 1% of the time
where the time goes in v4:
time: 49.5 us; the launch traced here: 49.2 us
  blocking collectives  28 us (57%)
  starting transfers between devices  10.4 us (21%)
  Pallas kernels  6.93 us (14%)
  waiting for transfers between devices  3.8 us (8%)
    all_to_all x1, blocking collectives, shards(): got = lax.all_to_all(joined, 'member', 0, 0, tiled=True)  19.5 us
    all_to_all x1, starting transfers between devices, shards(): owned = lax.all_to_all(owned, 'space', 0, 0, tiled=True)  10.4 us
    all_to_all x1, blocking collectives, shards(): parts = lax.all_to_all(local, 'tm', 0, 0, tiled=True)  8.48 us
    all_to_all x1, waiting for transfers between devices, shards(): owned = lax.all_to_all(owned, 'space', 0, 0, tiled=True)  3.8 us
    pallas_call x1, Pallas kernels, shards(): pl.pallas_call(lambda *refs: pick_kernel(scale, *refs), out_shape=(in_vme...  3.68 us
    pallas_call x1, Pallas kernels, shards(): pl.pallas_call(owned_kernel, out_shape=jax.ShapeDtypeStruct((tiles, LANES...  1.52 us
  transfers between devices with their start and end apart: 1, of which 1 were waited for; matrix products, arithmetic and copies ran while one was open for 0% of the time, Pallas kernels for 7%

profile of v4, /device:TPU:2, one launch (start us, length us, event | category | flops | bytes accessed | tf_op | source)
XLA Modules:
  0.0 49.2 jit_solution(13738417701023867637)
XLA Ops:
  0.0 0.0 copy-start
  0.0 1.5 %shard_map.74 = f32[16,128]{1,0:T(8,128)} custom-call(f32[2,16,32]{2,1,0:T(8,128)} %bitcast.10, f32[2,16,32]{2,1,0:T(8,128)} %bitcast.11, s32[2,16]{1,0:T(2,128)} %bitcast.12), custom_call_target="tpu_custom_call" | custom-call | tf_op jit(solution)/shard_map/pallas_call | solution.py:218
  1.5 10.4 %all-to-all-start = ((f32[16,1,128]{2,1,0:T(1,128)}), f32[16,1,128]{2,1,0:T(1,128)S(1)}, u32[]{:S(2)}, u32[]{:S(2)}) async-start(f32[16,1,128]{2,1,0:T(1,128)} %bitcast.6), calls=%async_computation | async-start | bytes 16384 | tf_op jit(solution)/shard_map/all_to_all | solution.py:235
  12.0 3.7 %shard_map.73 = (f32[64,128]{1,0:T(8,128)S(1)}, bf16[8,1024,128]{2,1,0:T(8,128)(2,1)S(1)}, s32[64,128]{1,0:T(8,128)S(1)}) custom-call(bf16[2,16,8192]{2,1,0:T(8,128)(2,1)} %ens_ref.1, f32[16,32]{1,0:T(8,128)} %refs_1_.3, s32[2,16,8,32]{3,2,1,0:T(8,128)} %bitcast.13, s32[2,16,8,32]{3,2,1,0:T(8,128)} %bitcast.14), custom_call_target="tpu_custom_call" | custom-call | flops 268435456 | bytes 4194304 | tf_op jit(solution)/shard_map/pallas_call | solution.py:236
  15.7 0.0 copy-start.1
  15.7 3.8 %all-to-all-done = f32[16,1,128]{2,1,0:T(1,128)S(1)} async-done(((f32[16,1,128]{2,1,0:T(1,128)}), f32[16,1,128]{2,1,0:T(1,128)S(1)}, u32[]{:S(2)}, u32[]{:S(2)}) %all-to-all-start) | async-done | bytes 8224 | tf_op jit(solution)/shard_map/all_to_all | solution.py:235
  19.5 0.1 shard_map.75
  19.6 19.5 %all_to_all.21.got_ref = f32[8,72,128]{2,1,0:T(8,128)S(1)} all-to-all(f32[8,72,128]{2,1,0:T(8,128)S(1)} %shard_map.75), channel_id=1, replica_groups=mesh['space'=16,'member'=8,'tm'=4] {'member'}, dimensions={0} | all-to-all | bytes 589824 | tf_op jit(solution)/shard_map/all_to_all | solution.py:270
  39.1 0.0 copy-done
  39.1 1.0 %shard_map.76 = f32[4,4,128]{2,1,0:T(4,128)S(1)} custom-call(bf16[2,16,8192]{2,1,0:T(8,128)(2,1)S(1)} %copy-done, f32[8,72,128]{2,1,0:T(8,128)S(1)} %all_to_all.21.got_ref, bf16[8,1024,128]{2,1,0:T(8,128)(2,1)S(1)} %get-tuple-element.9.hot_ref, s32[64,128]{1,0:T(8,128)S(1)} %get-tuple-element.10.high_ref), custom_call_target="tpu_custom_call" | custom-call | tf_op jit(solution)/shard_map/pallas_call | solution.py:271
  40.0 8.5 %all_to_all.22.refs_0_ = f32[4,4,128]{2,1,0:T(4,128)S(1)} all-to-all(f32[4,4,128]{2,1,0:T(4,128)S(1)} %shard_map.76), channel_id=1, replica_groups=mesh['space'=16,'member'=8,'tm'=4] {'tm'}, dimensions={0} | all-to-all | bytes 16384 | tf_op jit(solution)/shard_map/all_to_all | solution.py:278
  48.5 0.0 copy-done.1
  48.5 0.7 %shard_map.77 = f32[16,32]{1,0:T(8,128)} custom-call(f32[4,4,128]{2,1,0:T(4,128)S(1)} %all_to_all.22.refs_0_, f32[16,32]{1,0:T(8,128)S(1)} %copy-done.1), custom_call_target="tpu_custom_call" | custom-call | tf_op jit(solution)/shard_map/pallas_call | solution.py:279
Async XLA Ops:
  0.0 39.1 %copy-start = (bf16[2,16,8192]{2,1,0:T(8,128)(2,1)S(1)}, bf16[2,16,8192]{2,1,0:T(8,128)(2,1)}, u32[]{:S(2)}) copy-start(bf16[2,16,8192]{2,1,0:T(8,128)(2,1)} %ens_ref.1) | copy-start | bytes 1572868
  1.5 17.9 %all-to-all-start = ((f32[16,1,128]{2,1,0:T(1,128)}), f32[16,1,128]{2,1,0:T(1,128)S(1)}, u32[]{:S(2)}, u32[]{:S(2)}) async-start(f32[16,1,128]{2,1,0:T(1,128)} %bitcast.6), calls=%async_computation | async-start | bytes 16384 | tf_op jit(solution)/shard_map/all_to_all | solution.py:235
  15.7 32.9 %copy-start.1 = (f32[16,32]{1,0:T(8,128)S(1)}, f32[16,32]{1,0:T(8,128)}, u32[]{:S(2)}) copy-start(f32[16,32]{1,0:T(8,128)} %refs_1_.3) | copy-start | bytes 6148

commit v5 on v4

--- a/solution.py
+++ b/solution.py
@@ -9,10 +9,21 @@
 
 BLOCK = 256
 LANES = 128
+FIRST = {"space": 13, "member": 4, "tm": 2}
 VMEM = pl.BlockSpec(memory_space=pltpu.VMEM)
 HBM = pl.BlockSpec(memory_space=pltpu.HBM)
 PARAMS = pltpu.CompilerParams(vmem_limit_bytes=32 * 1024 * 1024)
 F32, BF16 = jnp.float32, jnp.bfloat16
+
+
+def turned(rows, first):
+    return jnp.concatenate([rows[first:], rows[:first]], axis=0) if first else rows
+
+
+def exchange(pieces, axis):
+    size = lax.axis_size(axis)
+    order = [(FIRST[axis] + i) % size for i in range(size)]
+    return lax.all_to_all(pieces, axis, 0, 0, tiled=True, axis_index_groups=[order])
 
 
 def fetch(sems, *pairs):
@@ -36,11 +47,12 @@
         columns.append(jnp.sum(jnp.where(diag, row, 0.0), axis=1, keepdims=True))
     copies[1].wait()
     copies[2].wait()
-    out_ref[...] = jnp.concatenate(
+    rows = jnp.concatenate(
         [jnp.where(lane < columns[t], var_ref[t], 0.0) for t in range(slots)]
         + [innov_ref[t] for t in range(slots)],
         axis=1,
     )
+    out_ref[...] = turned(rows, FIRST["space"])
 
 
 def hot_rows(ids, count):
@@ -112,10 +124,12 @@
     sublane = lax.broadcasted_iota(jnp.int32, (groups, LANES), 0)
     own_group = sublane == lax.axis_index("member")
 
+    owned = turned(owned_ref[...], (tiles - FIRST["space"]) % tiles)
+
     def aligned(source):
         total = None
         for q in range(quarters):
-            part = owned_ref[q * a_rows : (q + 1) * a_rows, :]
+            part = owned[q * a_rows : (q + 1) * a_rows]
             shift = (q - source) * cap % LANES
             part = pltpu.roll(part, shift, 1) if shift else part
             total = part if total is None else jnp.where(quarter == q, part, total)
@@ -148,7 +162,7 @@
             value = got_ref[0, at, :]
             for peer in range(1, groups):
                 value = value + got_ref[peer, at, :]
-            value = value * got_ref[:, rows + step, :]
+            value = value * turned(got_ref[:, rows + step, :], (groups - FIRST["member"]) % groups)
             upper = value.astype(BF16)
             lower = (value - upper.astype(F32)).astype(BF16)
             own = hot_rows(high_ref[at, :], highs).astype(BF16)
@@ -232,7 +246,7 @@
         in_hbm(inv_var.reshape(slots, tiles, cap)),
         in_hbm(obs_count.reshape(slots, tiles)),
     )
-    owned = lax.all_to_all(owned, "space", 0, 0, tiled=True)
+    owned = exchange(owned, "space")
     picks, hot, high = pl.pallas_call(
         lambda *refs: pick_kernel(scale, *refs),
         out_shape=(
@@ -267,7 +281,7 @@
         out_specs=VMEM,
         compiler_params=PARAMS,
     )(picks, owned)
-    got = lax.all_to_all(joined, "member", 0, 0, tiled=True)
+    got = exchange(joined, "member")
     local = pl.pallas_call(
         gradient_kernel,
         out_shape=jax.ShapeDtypeStruct((windows, members * blocks // LANES, LANES), F32),
@@ -275,7 +289,7 @@
         out_specs=VMEM,
         compiler_params=PARAMS,
     )(ens_pert, got, hot, high)
-    parts = lax.all_to_all(local, "tm", 0, 0, tiled=True)
+    parts = exchange(local, "tm")
     return pl.pallas_call(
         lambda *refs: finish_kernel(scale, *refs),
         out_shape=jax.ShapeDtypeStruct(weights.shape, F32),

time: 49.5 us -> 42.7 us (0.86)
  blocking collectives: 28 us -> 23.4 us
  waiting for transfers between devices: 3.8 us -> 0.37 us
  starting transfers between devices: 10.4 us -> 11.8 us
    all_to_all x2, blocking collectives: 28 us -> 23.4 us  [exchange(): lax.all_to_all(pieces, axis, 0, 0, tiled=True, axis_index_groups=[order])]
    all_to_all x1, waiting for transfers between devices: 3.8 us -> 0.37 us  [exchange(): lax.all_to_all(pieces, axis, 0, 0, tiled=True, axis_index_groups=[order])]
    all_to_all x1, starting transfers between devices: 10.4 us -> 11.8 us  [exchange(): lax.all_to_all(pieces, axis, 0, 0, tiled=True, axis_index_groups=[order])]
  transfers between devices with their start and end apart: 1 -> 1, of which waited for: 1 -> 1; matrix products, arithmetic and copies ran while one was open for 0% -> 0% of each run, Pallas kernels for 7% -> 9%
where the time goes in v5:
time: 42.7 us; the launch traced here: 42.5 us
  blocking collectives  23.4 us (55%)
  starting transfers between devices  11.8 us (28%)
  Pallas kernels  6.93 us (16%)
    all_to_all x2, blocking collectives, exchange(): lax.all_to_all(pieces, axis, 0, 0, tiled=True, axis_index_groups=[order])  23.4 us
    all_to_all x1, starting transfers between devices, exchange(): lax.all_to_all(pieces, axis, 0, 0, tiled=True, axis_index_groups=[order])  11.8 us
    pallas_call x1, Pallas kernels, shards(): pl.pallas_call(lambda *refs: pick_kernel(scale, *refs), out_shape=(in_vme...  3.68 us
    pallas_call x1, Pallas kernels, shards(): pl.pallas_call(owned_kernel, out_shape=jax.ShapeDtypeStruct((tiles, LANES...  1.52 us
    pallas_call x1, Pallas kernels, shards(): pl.pallas_call(gradient_kernel, out_shape=jax.ShapeDtypeStruct((windows,...  0.97 us
  transfers between devices with their start and end apart: 1, of which 1 were waited for; matrix products, arithmetic and copies ran while one was open for 0% of the time, Pallas kernels for 9%

profile of v5, /device:TPU:2, one launch (start us, length us, event | category | flops | bytes accessed | tf_op | source)
XLA Modules:
  0.0 42.5 jit_solution(6099103641323139197)
XLA Ops:
  0.0 0.0 copy-start
  0.0 1.5 %shard_map.74 = f32[16,128]{1,0:T(8,128)} custom-call(f32[2,16,32]{2,1,0:T(8,128)} %bitcast.10, f32[2,16,32]{2,1,0:T(8,128)} %bitcast.11, s32[2,16]{1,0:T(2,128)} %bitcast.12), custom_call_target="tpu_custom_call" | custom-call | tf_op jit(solution)/shard_map/pallas_call | solution.py:232
  1.5 11.8 %all-to-all-start = ((f32[16,1,128]{2,1,0:T(1,128)}), f32[16,1,128]{2,1,0:T(1,128)S(1)}, u32[]{:S(2)}, u32[]{:S(2)}) async-start(f32[16,1,128]{2,1,0:T(1,128)} %bitcast.6), calls=%async_computation | async-start | bytes 16384 | tf_op jit(solution)/shard_map/all_to_all | solution.py:26
  13.3 3.7 %shard_map.73 = (f32[64,128]{1,0:T(8,128)S(1)}, bf16[8,1024,128]{2,1,0:T(8,128)(2,1)S(1)}, s32[64,128]{1,0:T(8,128)S(1)}) custom-call(bf16[2,16,8192]{2,1,0:T(8,128)(2,1)} %ens_ref.1, f32[16,32]{1,0:T(8,128)} %refs_1_.3, s32[2,16,8,32]{3,2,1,0:T(8,128)} %bitcast.13, s32[2,16,8,32]{3,2,1,0:T(8,128)} %bitcast.14), custom_call_target="tpu_custom_call" | custom-call | flops 268435456 | bytes 4194304 | tf_op jit(solution)/shard_map/pallas_call | solution.py:250
  17.0 0.0 copy-start.1
  17.0 0.4 all-to-all-done
  17.4 0.1 shard_map.75
  17.5 15.7 %all_to_all.21.got_ref = f32[8,72,128]{2,1,0:T(8,128)S(1)} all-to-all(f32[8,72,128]{2,1,0:T(8,128)S(1)} %shard_map.75), channel_id=1, replica_groups={{16,20,24,28,0,4,8,12},{17,21,25,29,1,5,9,13},{18,22,26,30,2,6,10,14},{..., dimensions={0} | all-to-all | bytes 589824 | tf_op jit(solution)/shard_map/all_to_all | solution.py:26
  33.1 0.0 copy-done
  33.1 1.0 %shard_map.76 = f32[4,4,128]{2,1,0:T(4,128)S(1)} custom-call(bf16[2,16,8192]{2,1,0:T(8,128)(2,1)S(1)} %copy-done, f32[8,72,128]{2,1,0:T(8,128)S(1)} %all_to_all.21.got_ref, bf16[8,1024,128]{2,1,0:T(8,128)(2,1)S(1)} %get-tuple-element.9.hot_ref, s32[64,128]{1,0:T(8,128)S(1)} %get-tuple-element.10.high_ref), custom_call_target="tpu_custom_call" | custom-call | tf_op jit(solution)/shard_map/pallas_call | solution.py:285
  34.1 7.7 %all_to_all.22.refs_0_ = f32[4,4,128]{2,1,0:T(4,128)S(1)} all-to-all(f32[4,4,128]{2,1,0:T(4,128)S(1)} %shard_map.76), channel_id=1, replica_groups={{2,3,0,1},{6,7,4,5},{10,11,8,9},{14,15,12,13},{18,19,16,17},{22,23,20,2..., dimensions={0} | all-to-all | bytes 16384 | tf_op jit(solution)/shard_map/all_to_all | solution.py:26
  41.8 0.0 copy-done.1
  41.8 0.7 %shard_map.77 = f32[16,32]{1,0:T(8,128)} custom-call(f32[4,4,128]{2,1,0:T(4,128)S(1)} %all_to_all.22.refs_0_, f32[16,32]{1,0:T(8,128)S(1)} %copy-done.1), custom_call_target="tpu_custom_call" | custom-call | tf_op jit(solution)/shard_map/pallas_call | solution.py:293
Async XLA Ops:
  0.0 33.1 %copy-start = (bf16[2,16,8192]{2,1,0:T(8,128)(2,1)S(1)}, bf16[2,16,8192]{2,1,0:T(8,128)(2,1)}, u32[]{:S(2)}) copy-start(bf16[2,16,8192]{2,1,0:T(8,128)(2,1)} %ens_ref.1) | copy-start | bytes 1572868
  1.5 15.8 %all-to-all-start = ((f32[16,1,128]{2,1,0:T(1,128)}), f32[16,1,128]{2,1,0:T(1,128)S(1)}, u32[]{:S(2)}, u32[]{:S(2)}) async-start(f32[16,1,128]{2,1,0:T(1,128)} %bitcast.6), calls=%async_computation | async-start | bytes 16384 | tf_op jit(solution)/shard_map/all_to_all | solution.py:26
  17.0 24.8 %copy-start.1 = (f32[16,32]{1,0:T(8,128)S(1)}, f32[16,32]{1,0:T(8,128)}, u32[]{:S(2)}) copy-start(f32[16,32]{1,0:T(8,128)} %refs_1_.3) | copy-start | bytes 6148

commit v6 on v5

--- a/solution.py
+++ b/solution.py
@@ -9,7 +9,7 @@
 
 BLOCK = 256
 LANES = 128
-FIRST = {"space": 13, "member": 4, "tm": 2}
+FIRST = {"space": 11, "member": 5, "tm": 2}
 VMEM = pl.BlockSpec(memory_space=pltpu.VMEM)
 HBM = pl.BlockSpec(memory_space=pltpu.HBM)
 PARAMS = pltpu.CompilerParams(vmem_limit_bytes=32 * 1024 * 1024)
@@ -33,8 +33,20 @@
     return copies
 
 
-def owned_kernel(innov_hbm, var_hbm, count_hbm, out_ref, innov_ref, var_ref, count_ref, sems):
-    copies = fetch(sems, (count_hbm, count_ref), (var_hbm, var_ref), (innov_hbm, innov_ref))
+def owned_kernel(
+    innov_hbm, var_hbm, count_hbm, fb_hbm, fo_hbm, w_hbm, ens_hbm,
+    out_hbm, fb_ref, fo_ref, w_ref, ens_ref, innov_ref, var_ref, count_ref, out_ref, sems,
+):
+    copies = fetch(
+        sems,
+        (count_hbm, count_ref),
+        (var_hbm, var_ref),
+        (innov_hbm, innov_ref),
+        (fo_hbm, fo_ref),
+        (fb_hbm, fb_ref),
+        (w_hbm, w_ref),
+        (ens_hbm, ens_ref),
+    )
     slots, tiles, cap = innov_ref.shape
     diag = lax.broadcasted_iota(jnp.int32, (tiles, tiles), 0) == lax.broadcasted_iota(
         jnp.int32, (tiles, tiles), 1
@@ -53,6 +65,11 @@
         axis=1,
     )
     out_ref[...] = turned(rows, FIRST["space"])
+    write = pltpu.make_async_copy(out_ref, out_hbm, sems.at[len(copies)])
+    write.start()
+    for copy in copies[3:]:
+        copy.wait()
+    write.wait()
 
 
 def hot_rows(ids, count):
@@ -63,18 +80,14 @@
 
 
 def pick_kernel(
-    scale, ens_hbm, w_hbm, fb_hbm, fo_hbm, pick_ref, hot_ref, high_ref,
-    ens_ref, w_ref, fb_ref, fo_ref, low, field, split, sems,
+    scale, ens_ref, w_ref, fb_ref, fo_ref, pick_ref, hot_ref, high_ref, low, field, split
 ):
-    copies = fetch(sems, (fo_hbm, fo_ref), (fb_hbm, fb_ref), (w_hbm, w_ref), (ens_hbm, ens_ref))
     slots, members, cells = ens_ref.shape
     blocks = cells // BLOCK
     highs = cells // LANES
     tiles, groups, cap = fb_ref.shape[1:]
     quarters = LANES // cap
     a_rows = tiles // quarters
-    copies[0].wait()
-    copies[1].wait()
     for t in range(slots):
         for a in range(tiles):
             rows = pl.ds((t * a_rows + a % a_rows) * groups, groups)
@@ -83,8 +96,6 @@
             upper_half = offset >= LANES
             high_ref[rows, lanes] = fb_ref[t, a] + jnp.where(upper_half, blocks, 0)
             low[rows, lanes] = jnp.where(upper_half, offset - LANES, offset)
-    copies[2].wait()
-    copies[3].wait()
     w = w_ref[...].astype(BF16).astype(F32)
     for b in range(blocks):
         column = w[:, b : b + 1]
@@ -229,22 +240,33 @@
     rows = slots * tiles * groups * cap // LANES
     steps = rows // groups
     scale = 1.0 / math.sqrt(members * groups - 1)
-    owned = pl.pallas_call(
+    owned, fb, fo, w, ens = pl.pallas_call(
         owned_kernel,
-        out_shape=jax.ShapeDtypeStruct((tiles, LANES), F32),
-        in_specs=[HBM] * 3,
-        out_specs=VMEM,
+        out_shape=(
+            jax.ShapeDtypeStruct((tiles, LANES), F32),
+            in_vmem((slots, tiles, groups, cap), jnp.int32),
+            in_vmem((slots, tiles, groups, cap), jnp.int32),
+            in_vmem(weights.shape, F32),
+            in_vmem(ens_pert.shape, BF16),
+        ),
+        in_specs=[HBM] * 7,
+        out_specs=(HBM,) + (VMEM,) * 4,
         scratch_shapes=[
             pltpu.VMEM((slots, tiles, cap), F32),
             pltpu.VMEM((slots, tiles, cap), F32),
             pltpu.VMEM((slots, tiles), jnp.int32),
-            pltpu.SemaphoreType.DMA((3,)),
+            pltpu.VMEM((tiles, LANES), F32),
+            pltpu.SemaphoreType.DMA((8,)),
         ],
         compiler_params=PARAMS,
     )(
         in_hbm(innovation.reshape(slots, tiles, cap)),
         in_hbm(inv_var.reshape(slots, tiles, cap)),
         in_hbm(obs_count.reshape(slots, tiles)),
+        in_hbm(foot_block.reshape(slots, tiles, groups, cap)),
+        in_hbm(foot_offset.reshape(slots, tiles, groups, cap)),
+        in_hbm(weights),
+        in_hbm(ens_pert),
     )
     owned = exchange(owned, "space")
     picks, hot, high = pl.pallas_call(
@@ -254,26 +276,16 @@
             in_vmem((steps, groups * LANES, LANES), BF16),
             in_vmem((rows, LANES), jnp.int32),
         ),
-        in_specs=[HBM] * 4,
+        in_specs=[VMEM] * 4,
         out_specs=(VMEM,) * 3,
         scratch_shapes=[
-            pltpu.VMEM(ens_pert.shape, BF16),
-            pltpu.VMEM(weights.shape, F32),
-            pltpu.VMEM((slots, tiles, groups, cap), jnp.int32),
-            pltpu.VMEM((slots, tiles, groups, cap), jnp.int32),
             pltpu.VMEM((rows, LANES), jnp.int32),
             pltpu.VMEM((slots, highs, LANES), F32),
             pltpu.VMEM((slots, 2 * highs, LANES), BF16),
-            pltpu.SemaphoreType.DMA((4,)),
         ],
         compiler_params=PARAMS,
         cost_estimate=cost(4 * blocks * rows * LANES * BLOCK, 4 << 20),
-    )(
-        in_hbm(ens_pert),
-        in_hbm(weights),
-        in_hbm(foot_block.reshape(slots, tiles, groups, cap)),
-        in_hbm(foot_offset.reshape(slots, tiles, groups, cap)),
-    )
+    )(ens, w, fb, fo)
     joined = pl.pallas_call(
         join_kernel,
         out_shape=jax.ShapeDtypeStruct((groups, rows + steps, LANES), F32),
@@ -288,7 +300,7 @@
         in_specs=[VMEM] * 4,
         out_specs=VMEM,
         compiler_params=PARAMS,
-    )(ens_pert, got, hot, high)
+    )(ens, got, hot, high)
     parts = exchange(local, "tm")
     return pl.pallas_call(
         lambda *refs: finish_kernel(scale, *refs),
@@ -296,7 +308,7 @@
         in_specs=[VMEM] * 2,
         out_specs=VMEM,
         compiler_params=PARAMS,
-    )(parts, weights)
+    )(parts, w)
 
 
 def solution(mesh):

time: 42.7 us -> 42.3 us (level)
  Pallas kernels: 6.93 us -> 5.75 us
  starting transfers between devices: 11.8 us -> 12.4 us
    pallas_call x1, Pallas kernels: 3.68 us -> 2.51 us  [shards(): pl.pallas_call(lambda *refs: pick_kernel(scale, *refs), out_shape=(in_vme...]
    all_to_all x1, starting transfers between devices: 11.8 us -> 12.4 us  [exchange(): lax.all_to_all(pieces, axis, 0, 0, tiled=True, axis_index_groups=[order])]
  transfers between devices with their start and end apart: 1 -> 1, of which waited for: 1 -> 1; matrix products, arithmetic and copies ran while one was open for 0% -> 0% of each run, Pallas kernels for 9% -> 6%
where the time goes in v6:
time: 42.3 us; the launch traced here: 42.1 us
  blocking collectives  23.3 us (55%)
  starting transfers between devices  12.4 us (29%)
  Pallas kernels  5.75 us (14%)
  waiting for transfers between devices  0.65 us (2%)
    all_to_all x2, blocking collectives, exchange(): lax.all_to_all(pieces, axis, 0, 0, tiled=True, axis_index_groups=[order])  23.3 us
    all_to_all x1, starting transfers between devices, exchange(): lax.all_to_all(pieces, axis, 0, 0, tiled=True, axis_index_groups=[order])  12.4 us
    pallas_call x1, Pallas kernels, shards(): pl.pallas_call(lambda *refs: pick_kernel(scale, *refs), out_shape=(in_vme...  2.51 us
    pallas_call x1, Pallas kernels, shards(): pl.pallas_call(owned_kernel, out_shape=(jax.ShapeDtypeStruct((tiles, LANE...  1.5 us
    pallas_call x1, Pallas kernels, shards(): pl.pallas_call(gradient_kernel, out_shape=jax.ShapeDtypeStruct((windows,...  0.96 us
  transfers between devices with their start and end apart: 1, of which 1 were waited for; matrix products, arithmetic and copies ran while one was open for 0% of the time, Pallas kernels for 6%

profile of v6, /device:TPU:2, one launch (start us, length us, event | category | flops | bytes accessed | tf_op | source)
XLA Modules:
  0.0 42.1 jit_solution(8762248631070699140)
XLA Ops:
  0.0 1.5 %shard_map.73 = (f32[16,128]{1,0:T(8,128)}, s32[2,16,8,32]{3,2,1,0:T(8,128)S(1)}, s32[2,16,8,32]{3,2,1,0:T(8,128)S(1)}, f32[16,32]{1,0:T(8,128)S(1)}, bf16[2,16,8192]{2,1,0:T(8,128)(2,1)S(1)}) custom-call(f32[2,16,32]{2,1,0:T(8,128)} %bitcast.12, f32[2,16,32]{2,1,0:T(8,128)} %bitcast.13, s32[2,16]{1,0:T(2,128)} %bitcast.14, s32[2,16,8,32]{3,2,1,0:T(8,128)} %bitcast.10, ...), custom_call_target="tpu_custom_call" | custom-call | tf_op jit(solution)/shard_map/pallas_call | solution.py:243
  1.5 12.4 %all-to-all-start = ((f32[16,1,128]{2,1,0:T(1,128)}), f32[16,1,128]{2,1,0:T(1,128)S(1)}, u32[]{:S(2)}, u32[]{:S(2)}) async-start(f32[16,1,128]{2,1,0:T(1,128)} %bitcast.6), calls=%async_computation | async-start | bytes 16384 | tf_op jit(solution)/shard_map/all_to_all | solution.py:26
  13.9 2.5 %shard_map.74 = (f32[64,128]{1,0:T(8,128)S(1)}, bf16[8,1024,128]{2,1,0:T(8,128)(2,1)S(1)}, s32[64,128]{1,0:T(8,128)S(1)}) custom-call(bf16[2,16,8192]{2,1,0:T(8,128)(2,1)S(1)} %get-tuple-element.13.refs_0_.ens_ref, f32[16,32]{1,0:T(8,128)S(1)} %get-tuple-element.14.refs_1_, s32[2,16,8,32]{3,2,1,0:T(8,128)S(1)} %get-tuple-element.15.refs_2_, ...), custom_call_target="tpu_custom_call" | custom-call | flops 268435456 | bytes 4194304 | tf_op jit(solution)/shard_map/pallas_call | solution.py:272
  16.5 0.6 %all-to-all-done = f32[16,1,128]{2,1,0:T(1,128)S(1)} async-done(((f32[16,1,128]{2,1,0:T(1,128)}), f32[16,1,128]{2,1,0:T(1,128)S(1)}, u32[]{:S(2)}, u32[]{:S(2)}) %all-to-all-start) | async-done | bytes 8224 | tf_op jit(solution)/shard_map/all_to_all | solution.py:26
  17.1 0.1 shard_map.75
  17.2 15.6 %all_to_all.21.got_ref = f32[8,72,128]{2,1,0:T(8,128)S(1)} all-to-all(f32[8,72,128]{2,1,0:T(8,128)S(1)} %shard_map.75), channel_id=1, replica_groups={{20,24,28,0,4,8,12,16},{21,25,29,1,5,9,13,17},{22,26,30,2,6,10,14,18},{..., dimensions={0} | all-to-all | bytes 589824 | tf_op jit(solution)/shard_map/all_to_all | solution.py:26
  32.8 1.0 %shard_map.76 = f32[4,4,128]{2,1,0:T(4,128)S(1)} custom-call(bf16[2,16,8192]{2,1,0:T(8,128)(2,1)S(1)} %get-tuple-element.13.refs_0_.ens_ref, f32[8,72,128]{2,1,0:T(8,128)S(1)} %all_to_all.21.got_ref, bf16[8,1024,128]{2,1,0:T(8,128)(2,1)S(1)} %get-tuple-element.19.hot_ref, s32[64,128]{1,0:T(8,128)S(1)} %get-tuple-element.20.high_ref), custom_call_target="tpu_custom_call" | custom-call | tf_op jit(solution)/shard_map/pallas_call | solution.py:297
  33.8 7.7 %all_to_all.22.refs_0_ = f32[4,4,128]{2,1,0:T(4,128)S(1)} all-to-all(f32[4,4,128]{2,1,0:T(4,128)S(1)} %shard_map.76), channel_id=1, replica_groups={{2,3,0,1},{6,7,4,5},{10,11,8,9},{14,15,12,13},{18,19,16,17},{22,23,20,2..., dimensions={0} | all-to-all | bytes 16384 | tf_op jit(solution)/shard_map/all_to_all | solution.py:26
  41.4 0.7 %shard_map.77 = f32[16,32]{1,0:T(8,128)} custom-call(f32[4,4,128]{2,1,0:T(4,128)S(1)} %all_to_all.22.refs_0_, f32[16,32]{1,0:T(8,128)S(1)} %get-tuple-element.14.refs_1_), custom_call_target="tpu_custom_call" | custom-call | tf_op jit(solution)/shard_map/pallas_call | solution.py:305
Async XLA Ops:
  1.5 15.6 %all-to-all-start = ((f32[16,1,128]{2,1,0:T(1,128)}), f32[16,1,128]{2,1,0:T(1,128)S(1)}, u32[]{:S(2)}, u32[]{:S(2)}) async-start(f32[16,1,128]{2,1,0:T(1,128)} %bitcast.6), calls=%async_computation | async-start | bytes 16384 | tf_op jit(solution)/shard_map/all_to_all | solution.py:26

commit v7 on v6

--- a/solution.py
+++ b/solution.py
@@ -37,16 +37,7 @@
     innov_hbm, var_hbm, count_hbm, fb_hbm, fo_hbm, w_hbm, ens_hbm,
     out_hbm, fb_ref, fo_ref, w_ref, ens_ref, innov_ref, var_ref, count_ref, out_ref, sems,
 ):
-    copies = fetch(
-        sems,
-        (count_hbm, count_ref),
-        (var_hbm, var_ref),
-        (innov_hbm, innov_ref),
-        (fo_hbm, fo_ref),
-        (fb_hbm, fb_ref),
-        (w_hbm, w_ref),
-        (ens_hbm, ens_ref),
-    )
+    copies = fetch(sems, (count_hbm, count_ref), (var_hbm, var_ref), (innov_hbm, innov_ref))
     slots, tiles, cap = innov_ref.shape
     diag = lax.broadcasted_iota(jnp.int32, (tiles, tiles), 0) == lax.broadcasted_iota(
         jnp.int32, (tiles, tiles), 1
@@ -59,15 +50,19 @@
         columns.append(jnp.sum(jnp.where(diag, row, 0.0), axis=1, keepdims=True))
     copies[1].wait()
     copies[2].wait()
-    rows = jnp.concatenate(
-        [jnp.where(lane < columns[t], var_ref[t], 0.0) for t in range(slots)]
-        + [innov_ref[t] for t in range(slots)],
-        axis=1,
-    )
-    out_ref[...] = turned(rows, FIRST["space"])
-    write = pltpu.make_async_copy(out_ref, out_hbm, sems.at[len(copies)])
+    first = FIRST["space"]
+    for t in range(slots):
+        held = jnp.where(lane < columns[t], var_ref[t], 0.0)
+        out_ref[:, t * cap : (t + 1) * cap] = turned(held, first)
+        given = turned(innov_ref[t], first)
+        out_ref[:, (slots + t) * cap : (slots + t + 1) * cap] = given
+    write = pltpu.make_async_copy(out_ref, out_hbm, sems.at[7])
     write.start()
-    for copy in copies[3:]:
+    pairs = ((fo_hbm, fo_ref), (fb_hbm, fb_ref), (w_hbm, w_ref), (ens_hbm, ens_ref))
+    rest = [pltpu.make_async_copy(src, dst, sems.at[3 + i]) for i, (src, dst) in enumerate(pairs)]
+    for copy in rest:
+        copy.start()
+    for copy in rest:
         copy.wait()
     write.wait()
 

time: 42.3 us -> 43 us (1.017)
  Pallas kernels: 5.75 us -> 6.35 us
    pallas_call x1, Pallas kernels: 1.5 us -> 2.11 us  [shards(): pl.pallas_call(owned_kernel, out_shape=(jax.ShapeDtypeStruct((tiles, LANE...]
where the time goes in v7:
time: 43 us; the launch traced here: 42.7 us
  blocking collectives  23.3 us (54%)
  starting transfers between devices  12.4 us (29%)
  Pallas kernels  6.35 us (15%)
  waiting for transfers between devices  0.64 us (1%)
    all_to_all x2, blocking collectives, exchange(): lax.all_to_all(pieces, axis, 0, 0, tiled=True, axis_index_groups=[order])  23.3 us
    all_to_all x1, starting transfers between devices, exchange(): lax.all_to_all(pieces, axis, 0, 0, tiled=True, axis_index_groups=[order])  12.4 us
    pallas_call x1, Pallas kernels, shards(): pl.pallas_call(lambda *refs: pick_kernel(scale, *refs), out_shape=(in_vme...  2.51 us
    pallas_call x1, Pallas kernels, shards(): pl.pallas_call(owned_kernel, out_shape=(jax.ShapeDtypeStruct((tiles, LANE...  2.11 us
    pallas_call x1, Pallas kernels, shards(): pl.pallas_call(gradient_kernel, out_shape=jax.ShapeDtypeStruct((windows,...  0.96 us
  transfers between devices with their start and end apart: 1, of which 1 were waited for; matrix products, arithmetic and copies ran while one was open for 0% of the time, Pallas kernels for 6%

profile of v7, /device:TPU:2, one launch (start us, length us, event | category | flops | bytes accessed | tf_op | source)
XLA Modules:
  0.0 42.7 jit_solution(7158803918136323975)
XLA Ops:
  0.0 2.1 %shard_map.73 = (f32[16,128]{1,0:T(8,128)}, s32[2,16,8,32]{3,2,1,0:T(8,128)S(1)}, s32[2,16,8,32]{3,2,1,0:T(8,128)S(1)}, f32[16,32]{1,0:T(8,128)S(1)}, bf16[2,16,8192]{2,1,0:T(8,128)(2,1)S(1)}) custom-call(f32[2,16,32]{2,1,0:T(8,128)} %bitcast.12, f32[2,16,32]{2,1,0:T(8,128)} %bitcast.13, s32[2,16]{1,0:T(2,128)} %bitcast.14, s32[2,16,8,32]{3,2,1,0:T(8,128)} %bitcast.10, ...), custom_call_target="tpu_custom_call" | custom-call | tf_op jit(solution)/shard_map/pallas_call | solution.py:238
  2.1 12.4 %all-to-all-start = ((f32[16,1,128]{2,1,0:T(1,128)}), f32[16,1,128]{2,1,0:T(1,128)S(1)}, u32[]{:S(2)}, u32[]{:S(2)}) async-start(f32[16,1,128]{2,1,0:T(1,128)} %bitcast.6), calls=%async_computation | async-start | bytes 16384 | tf_op jit(solution)/shard_map/all_to_all | solution.py:26
  14.5 2.5 %shard_map.74 = (f32[64,128]{1,0:T(8,128)S(1)}, bf16[8,1024,128]{2,1,0:T(8,128)(2,1)S(1)}, s32[64,128]{1,0:T(8,128)S(1)}) custom-call(bf16[2,16,8192]{2,1,0:T(8,128)(2,1)S(1)} %get-tuple-element.13.refs_0_.ens_ref, f32[16,32]{1,0:T(8,128)S(1)} %get-tuple-element.14.refs_1_, s32[2,16,8,32]{3,2,1,0:T(8,128)S(1)} %get-tuple-element.15.refs_2_, ...), custom_call_target="tpu_custom_call" | custom-call | flops 268435456 | bytes 4194304 | tf_op jit(solution)/shard_map/pallas_call | solution.py:267
  17.1 0.6 %all-to-all-done = f32[16,1,128]{2,1,0:T(1,128)S(1)} async-done(((f32[16,1,128]{2,1,0:T(1,128)}), f32[16,1,128]{2,1,0:T(1,128)S(1)}, u32[]{:S(2)}, u32[]{:S(2)}) %all-to-all-start) | async-done | bytes 8224 | tf_op jit(solution)/shard_map/all_to_all | solution.py:26
  17.7 0.1 shard_map.75
  17.8 15.6 %all_to_all.21.got_ref = f32[8,72,128]{2,1,0:T(8,128)S(1)} all-to-all(f32[8,72,128]{2,1,0:T(8,128)S(1)} %shard_map.75), channel_id=1, replica_groups={{20,24,28,0,4,8,12,16},{21,25,29,1,5,9,13,17},{22,26,30,2,6,10,14,18},{..., dimensions={0} | all-to-all | bytes 589824 | tf_op jit(solution)/shard_map/all_to_all | solution.py:26
  33.4 1.0 %shard_map.76 = f32[4,4,128]{2,1,0:T(4,128)S(1)} custom-call(bf16[2,16,8192]{2,1,0:T(8,128)(2,1)S(1)} %get-tuple-element.13.refs_0_.ens_ref, f32[8,72,128]{2,1,0:T(8,128)S(1)} %all_to_all.21.got_ref, bf16[8,1024,128]{2,1,0:T(8,128)(2,1)S(1)} %get-tuple-element.19.hot_ref, s32[64,128]{1,0:T(8,128)S(1)} %get-tuple-element.20.high_ref), custom_call_target="tpu_custom_call" | custom-call | tf_op jit(solution)/shard_map/pallas_call | solution.py:292
  34.4 7.7 %all_to_all.22.refs_0_ = f32[4,4,128]{2,1,0:T(4,128)S(1)} all-to-all(f32[4,4,128]{2,1,0:T(4,128)S(1)} %shard_map.76), channel_id=1, replica_groups={{2,3,0,1},{6,7,4,5},{10,11,8,9},{14,15,12,13},{18,19,16,17},{22,23,20,2..., dimensions={0} | all-to-all | bytes 16384 | tf_op jit(solution)/shard_map/all_to_all | solution.py:26
  42.0 0.7 %shard_map.77 = f32[16,32]{1,0:T(8,128)} custom-call(f32[4,4,128]{2,1,0:T(4,128)S(1)} %all_to_all.22.refs_0_, f32[16,32]{1,0:T(8,128)S(1)} %get-tuple-element.14.refs_1_), custom_call_target="tpu_custom_call" | custom-call | tf_op jit(solution)/shard_map/pallas_call | solution.py:300
Async XLA Ops:
  2.1 15.6 %all-to-all-start = ((f32[16,1,128]{2,1,0:T(1,128)}), f32[16,1,128]{2,1,0:T(1,128)S(1)}, u32[]{:S(2)}, u32[]{:S(2)}) async-start(f32[16,1,128]{2,1,0:T(1,128)} %bitcast.6), calls=%async_computation | async-start | bytes 16384 | tf_op jit(solution)/shard_map/all_to_all | solution.py:26

commit v8 on v6

--- a/solution.py
+++ b/solution.py
@@ -59,12 +59,12 @@
         columns.append(jnp.sum(jnp.where(diag, row, 0.0), axis=1, keepdims=True))
     copies[1].wait()
     copies[2].wait()
-    rows = jnp.concatenate(
-        [jnp.where(lane < columns[t], var_ref[t], 0.0) for t in range(slots)]
-        + [innov_ref[t] for t in range(slots)],
-        axis=1,
-    )
-    out_ref[...] = turned(rows, FIRST["space"])
+    first = FIRST["space"]
+    for t in range(slots):
+        held = jnp.where(lane < columns[t], var_ref[t], 0.0)
+        out_ref[:, t * cap : (t + 1) * cap] = turned(held, first)
+        given = turned(innov_ref[t], first)
+        out_ref[:, (slots + t) * cap : (slots + t + 1) * cap] = given
     write = pltpu.make_async_copy(out_ref, out_hbm, sems.at[len(copies)])
     write.start()
     for copy in copies[3:]:

time: 42.3 us -> 42.3 us (level)
  no operation moved by 1% of the time
where the time goes in v8:
time: 42.3 us; the launch traced here: 42.1 us
  blocking collectives  23.3 us (55%)
  starting transfers between devices  12.4 us (29%)
  Pallas kernels  5.75 us (14%)
  waiting for transfers between devices  0.65 us (2%)
    all_to_all x2, blocking collectives, exchange(): lax.all_to_all(pieces, axis, 0, 0, tiled=True, axis_index_groups=[order])  23.3 us
    all_to_all x1, starting transfers between devices, exchange(): lax.all_to_all(pieces, axis, 0, 0, tiled=True, axis_index_groups=[order])  12.4 us
    pallas_call x1, Pallas kernels, shards(): pl.pallas_call(lambda *refs: pick_kernel(scale, *refs), out_shape=(in_vme...  2.51 us
    pallas_call x1, Pallas kernels, shards(): pl.pallas_call(owned_kernel, out_shape=(jax.ShapeDtypeStruct((tiles, LANE...  1.5 us
    pallas_call x1, Pallas kernels, shards(): pl.pallas_call(gradient_kernel, out_shape=jax.ShapeDtypeStruct((windows,...  0.96 us
  transfers between devices with their start and end apart: 1, of which 1 were waited for; matrix products, arithmetic and copies ran while one was open for 0% of the time, Pallas kernels for 6%

profile of v8, /device:TPU:2, one launch (start us, length us, event | category | flops | bytes accessed | tf_op | source)
XLA Modules:
  0.0 42.1 jit_solution(15468754114175715881)
XLA Ops:
  0.0 1.5 %shard_map.73 = (f32[16,128]{1,0:T(8,128)}, s32[2,16,8,32]{3,2,1,0:T(8,128)S(1)}, s32[2,16,8,32]{3,2,1,0:T(8,128)S(1)}, f32[16,32]{1,0:T(8,128)S(1)}, bf16[2,16,8192]{2,1,0:T(8,128)(2,1)S(1)}) custom-call(f32[2,16,32]{2,1,0:T(8,128)} %bitcast.12, f32[2,16,32]{2,1,0:T(8,128)} %bitcast.13, s32[2,16]{1,0:T(2,128)} %bitcast.14, s32[2,16,8,32]{3,2,1,0:T(8,128)} %bitcast.10, ...), custom_call_target="tpu_custom_call" | custom-call | tf_op jit(solution)/shard_map/pallas_call | solution.py:243
  1.5 12.4 %all-to-all-start = ((f32[16,1,128]{2,1,0:T(1,128)}), f32[16,1,128]{2,1,0:T(1,128)S(1)}, u32[]{:S(2)}, u32[]{:S(2)}) async-start(f32[16,1,128]{2,1,0:T(1,128)} %bitcast.6), calls=%async_computation | async-start | bytes 16384 | tf_op jit(solution)/shard_map/all_to_all | solution.py:26
  13.9 2.5 %shard_map.74 = (f32[64,128]{1,0:T(8,128)S(1)}, bf16[8,1024,128]{2,1,0:T(8,128)(2,1)S(1)}, s32[64,128]{1,0:T(8,128)S(1)}) custom-call(bf16[2,16,8192]{2,1,0:T(8,128)(2,1)S(1)} %get-tuple-element.13.refs_0_.ens_ref, f32[16,32]{1,0:T(8,128)S(1)} %get-tuple-element.14.refs_1_, s32[2,16,8,32]{3,2,1,0:T(8,128)S(1)} %get-tuple-element.15.refs_2_, ...), custom_call_target="tpu_custom_call" | custom-call | flops 268435456 | bytes 4194304 | tf_op jit(solution)/shard_map/pallas_call | solution.py:272
  16.5 0.6 %all-to-all-done = f32[16,1,128]{2,1,0:T(1,128)S(1)} async-done(((f32[16,1,128]{2,1,0:T(1,128)}), f32[16,1,128]{2,1,0:T(1,128)S(1)}, u32[]{:S(2)}, u32[]{:S(2)}) %all-to-all-start) | async-done | bytes 8224 | tf_op jit(solution)/shard_map/all_to_all | solution.py:26
  17.1 0.1 shard_map.75
  17.2 15.6 %all_to_all.21.got_ref = f32[8,72,128]{2,1,0:T(8,128)S(1)} all-to-all(f32[8,72,128]{2,1,0:T(8,128)S(1)} %shard_map.75), channel_id=1, replica_groups={{20,24,28,0,4,8,12,16},{21,25,29,1,5,9,13,17},{22,26,30,2,6,10,14,18},{..., dimensions={0} | all-to-all | bytes 589824 | tf_op jit(solution)/shard_map/all_to_all | solution.py:26
  32.8 1.0 %shard_map.76 = f32[4,4,128]{2,1,0:T(4,128)S(1)} custom-call(bf16[2,16,8192]{2,1,0:T(8,128)(2,1)S(1)} %get-tuple-element.13.refs_0_.ens_ref, f32[8,72,128]{2,1,0:T(8,128)S(1)} %all_to_all.21.got_ref, bf16[8,1024,128]{2,1,0:T(8,128)(2,1)S(1)} %get-tuple-element.19.hot_ref, s32[64,128]{1,0:T(8,128)S(1)} %get-tuple-element.20.high_ref), custom_call_target="tpu_custom_call" | custom-call | tf_op jit(solution)/shard_map/pallas_call | solution.py:297
  33.8 7.7 %all_to_all.22.refs_0_ = f32[4,4,128]{2,1,0:T(4,128)S(1)} all-to-all(f32[4,4,128]{2,1,0:T(4,128)S(1)} %shard_map.76), channel_id=1, replica_groups={{2,3,0,1},{6,7,4,5},{10,11,8,9},{14,15,12,13},{18,19,16,17},{22,23,20,2..., dimensions={0} | all-to-all | bytes 16384 | tf_op jit(solution)/shard_map/all_to_all | solution.py:26
  41.4 0.7 %shard_map.77 = f32[16,32]{1,0:T(8,128)} custom-call(f32[4,4,128]{2,1,0:T(4,128)S(1)} %all_to_all.22.refs_0_, f32[16,32]{1,0:T(8,128)S(1)} %get-tuple-element.14.refs_1_), custom_call_target="tpu_custom_call" | custom-call | tf_op jit(solution)/shard_map/pallas_call | solution.py:305
Async XLA Ops:
  1.5 15.6 %all-to-all-start = ((f32[16,1,128]{2,1,0:T(1,128)}), f32[16,1,128]{2,1,0:T(1,128)S(1)}, u32[]{:S(2)}, u32[]{:S(2)}) async-start(f32[16,1,128]{2,1,0:T(1,128)} %bitcast.6), calls=%async_computation | async-start | bytes 16384 | tf_op jit(solution)/shard_map/all_to_all | solution.py:26
